TPU v7x, 512 devices: a whole 4x8x8 slice. The times are simulated.
512 devices in a mesh: hid: 64 (over z, y), wid: 8 (over x, core).
Axes of the slice: x: 4, y: 8, z: 8, core: 2. Of those that a mesh axis runs over, the one named last changes fastest.
Arguments:
- tokens: bfloat16 [256, 12288], P('hid', 'wid'), may hold values from -6 to 6
- out_grad: bfloat16 [256, 12288], P('hid', 'wid'), may hold values from -6 to 6
- up_tiles: bfloat16 [64, 8, 18, 128, 128], P('hid', 'wid'), may hold values from -0.109375 to 0.109375
- down_tiles: bfloat16 [64, 8, 18, 128, 128], P('hid', 'wid'), may hold values from -0.0546875 to 0.0546875
- up_slots: int32 [64, 8, 18], P('hid', 'wid'), may hold values from 0 to 71, as said below
- down_slots: int32 [64, 8, 18], P('hid', 'wid'), may hold values from 0 to 71, as said below
Outputs:
- mixed: bfloat16 [256, 12288], P('hid', 'wid')
- grad_tokens: bfloat16 [256, 12288], P('hid', 'wid')
- grad_up: float32 [64, 8, 18, 128, 128], P('hid', 'wid')
- grad_down: float32 [64, 8, 18, 128, 128], P('hid', 'wid')
Inputs may be any that keep to these rules, and one draw needn't show every extreme that they name: `up_slots`: on each device the 18 positions are distinct and ascending, a quarter of the 72 positions. `down_slots`: on each device the 18 positions are distinct and ascending, a quarter of the 72 positions.
All inputs are finite; a program needn't handle non-finite values.
Results may differ from a plain program's by a relative error of at most 0.0049.
Values may be sent and summed in bfloat16 or wider, within the bound.
A program may use at most 64 MiB of HBM per device.

v0:
```python
import jax
import jax.numpy as jnp
from jax import lax
from jax.sharding import PartitionSpec as P

FF = 49152


highest = lax.Precision.HIGHEST
root_coef = 0.7978845608028654
cubic_coef = 0.044715


def gelu_value(value):
    inner = jnp.tanh(root_coef * (value + cubic_coef * value * value * value))
    return 0.5 * value * (1.0 + inner)


def gelu_slope(value):
    inner = jnp.tanh(root_coef * (value + cubic_coef * value * value * value))
    return 0.5 * (1.0 + inner) + 0.5 * value * (1.0 - inner * inner) * root_coef * (
        1.0 + 3.0 * cubic_coef * value * value
    )


def one_hot(values, count):
    return (values[:, None] == jnp.arange(count, dtype=jnp.int32)[None, :]).astype(jnp.float32)


def per_device(tokens, out_grad, up_tiles, down_tiles, up_slots, down_slots):
    tile_size = up_tiles.shape[-1]
    up_tile = up_tiles[0, 0]
    down_tile = down_tiles[0, 0]
    up_slot = up_slots[0, 0]
    down_slot = down_slots[0, 0]
    row_tiles = tokens.shape[1] // tile_size
    hid_blocks = FF // (tile_size * lax.axis_size("hid"))
    gathered, gathered_grad = (
        lax.all_gather(tokens, "hid", axis=0, tiled=True),
        lax.all_gather(out_grad, "hid", axis=0, tiled=True),
    )
    token_count = gathered.shape[0]
    up_rows = up_slot // hid_blocks
    up_block = up_slot % hid_blocks
    down_block = down_slot // row_tiles
    down_cols = down_slot % row_tiles
    up_hot = one_hot(up_block, hid_blocks)
    row_hot = one_hot(up_rows, row_tiles)
    down_hot = one_hot(down_block, hid_blocks)
    col_hot = one_hot(down_cols, row_tiles)
    x_tiles = jnp.take(gathered.reshape(token_count, row_tiles, tile_size), up_rows, axis=1)
    grad_tiles = jnp.take(
        gathered_grad.reshape(token_count, row_tiles, tile_size), down_cols, axis=1
    )
    up_prod = jnp.einsum("tnk,nkj->tnj", x_tiles, up_tile, preferred_element_type=jnp.float32)
    pre_part = jnp.einsum("tnj,nb->tbj", up_prod, up_hot, precision=highest).reshape(
        token_count, hid_blocks * tile_size
    )
    back_prod = jnp.einsum(
        "tnj,nkj->tnk", grad_tiles, down_tile, preferred_element_type=jnp.float32
    )
    back_part = jnp.einsum("tnk,nb->tbk", back_prod, down_hot, precision=highest).reshape(
        token_count, hid_blocks * tile_size
    )
    pre_sum, back_sum = lax.psum((pre_part, back_part), "wid")
    hidden = gelu_value(pre_sum).astype(jnp.bfloat16)
    delta_rows = (back_sum * gelu_slope(pre_sum)).astype(jnp.bfloat16)
    count = tokens.shape[0] * lax.axis_size("hid")
    picked_rows = hidden
    picked = jnp.take(picked_rows.reshape(count, hid_blocks, tile_size), down_block, axis=1)
    product = jnp.einsum("tnk,nkj->tnj", picked, down_tile, preferred_element_type=jnp.float32)
    mixed = lax.psum_scatter(
        jnp.einsum("tnj,nc->tcj", product, col_hot, precision=highest).reshape(
            count, row_tiles * tile_size
        ),
        "hid",
        scatter_dimension=0,
        tiled=True,
    ).astype(jnp.bfloat16)
    count = tokens.shape[0] * lax.axis_size("hid")
    picked_rows = delta_rows
    picked = jnp.take(picked_rows.reshape(count, hid_blocks, tile_size), up_block, axis=1)
    product = jnp.einsum("tnj,nkj->tnk", picked, up_tile, preferred_element_type=jnp.float32)
    grad_tokens = lax.psum_scatter(
        jnp.einsum("tnk,nr->trk", product, row_hot, precision=highest).reshape(
            count, row_tiles * tile_size
        ),
        "hid",
        scatter_dimension=0,
        tiled=True,
    ).astype(jnp.bfloat16)
    hidden_tiles = jnp.take(hidden.reshape(token_count, hid_blocks, tile_size), down_block, axis=1)
    delta_tiles = jnp.take(delta_rows.reshape(token_count, hid_blocks, tile_size), up_block, axis=1)
    grad_up = jnp.einsum("tnk,tnj->nkj", x_tiles, delta_tiles, preferred_element_type=jnp.float32)
    grad_down = jnp.einsum(
        "tnk,tnj->nkj", hidden_tiles, grad_tiles, preferred_element_type=jnp.float32
    )
    return (mixed, grad_tokens, grad_up[None, None], grad_down[None, None])


def solution(mesh):
    in_specs = (
        P("hid", "wid"),
        P("hid", "wid"),
        P("hid", "wid", None, None, None),
        P("hid", "wid", None, None, None),
        P("hid", "wid", None),
        P("hid", "wid", None),
    )
    out_specs = (
        P("hid", "wid"),
        P("hid", "wid"),
        P("hid", "wid", None, None, None),
        P("hid", "wid", None, None, None),
    )
    return jax.shard_map(
        per_device, mesh=mesh, in_specs=in_specs, out_specs=out_specs, check_vma=False
    )
```

profile of v0, /device:TPU:6, one launch (start us, length us, event | category | flops | bytes accessed | tf_op | source)
XLA Modules:
  0.0 552.0 jit_solution(17029858678319150202)
XLA Ops:
  7.2 0.0 copy-start
  7.2 0.0 all-reduce.7.cloned.1.call-start
  7.2 0.7 compare_and_fusion
  8.0 0.7 compare_and_fusion.2
  8.7 57.5 %all-gather = bf16[64,4,1536]{2,1,0:T(4,128)(2,1)S(1)} all-gather(bf16[1,4,1536]{2,1,0:T(4,128)(2,1)} %bitcast.107), channel_id=1, replica_groups=mesh['hid'=64,'wid'=8] {'hid'}, dimensions={0}, use_global_device_ids=true | all-gather | bytes 798720 | tf_op jit(solution)/shard_map/all_gather | solution.py:39
  66.2 0.5 reshape.108
  66.7 0.0 copy-start.7
  66.7 0.2 copy.22
  66.9 0.5 copy-done.7
  67.4 48.8 %all-gather.1 = bf16[64,4,1536]{2,1,0:T(4,128)(2,1)S(1)} all-gather(bf16[1,4,1536]{2,1,0:T(4,128)(2,1)S(1)} %bitcast.108), channel_id=1, replica_groups=mesh['hid'=64,'wid'=8] {'hid'}, dimensions={0}, use_global_device_ids=true | all-gather | bytes 798720 | tf_op jit(solution)/shard_map/all_gather | solution.py:40
  116.2 0.5 reshape.112
  116.7 0.2 copy.28
  116.9 0.8 gather_fusion.2
  117.7 0.0 copy-start.2
  117.7 2.0 convolution_bitcast_fusion.1
  119.7 0.0 copy-done.2
  119.7 2.3 fusion.17
  122.1 1.2 copy.30
  123.3 0.8 gather_fusion
  124.1 0.0 copy-done
  124.1 0.5 convolution_bitcast_fusion.3
  124.6 2.3 fusion.14
  127.0 1.2 copy.24
  128.2 0.0 all-reduce.7.cloned.1.call-update
  128.2 1.3 dynamic-slice
  130.2 65.9 %all-reduce.7.cloned.1.call-done = (f32[256,768]{0,1:T(8,128)}, f32[256,768]{0,1:T(8,128)}) async-done(((f32[256,768]{0,1:T(8,128)}, f32[256,768]{0,1:T(8,128)}), (f32[256,768]{0,1:T(8,128)}, f32[256,768]{0,1:T(8,128)})) %all-reduce.7.cloned.1.call-update) | async-done | bytes 1572880 | tf_op jit(solution)/shard_map/psum | solution.py:65
  196.1 2.7 fusion.34
  198.7 0.2 copy.31
  199.0 0.8 gather_fusion.3
  199.8 0.0 copy-start.3
  199.8 1.0 copy-done.3
  200.8 1.6 convolution_bitcast_fusion.5
  202.4 1.8 convolution_bitcast_fusion
  204.2 1.2 copy.25
  205.4 1.8 gather_fusion.1
  207.2 3.4 convolution_bitcast_fusion.4
  210.6 0.0 copy-done.4
  210.6 2.1 convolution_bitcast_fusion.2
  212.7 3.8 fusion.11
  216.6 2.9 copy.33
  219.5 0.0 copy-done.1
  219.5 3.9 fusion.8
  223.3 2.9 copy.27
  226.2 0.0 copy-done.5
  226.2 316.1 %all-reduce.8 = (bf16[256,1536]{0,1:T(8,128)(2,1)S(1)}, bf16[256,1536]{0,1:T(8,128)(2,1)}) all-reduce(f32[256,1536]{0,1:T(8,128)} %bitcast.102, f32[256,1536]{0,1:T(8,128)S(1)} %bitcast.101), channel_id=2, replica_groups=mesh['hid'=64,'wid'=8] {'hid'}, use_global_device_ids=true, to_apply=%region_1.4.clone | all-reduce | flops 786432 | bytes 4718592
  542.3 1.3 dynamic-slice_convert_fusion
  543.6 0.8 copy.37
  544.4 0.8 copy.36
  (13 shorter events, 0.0 us)
Async XLA Ops:
  7.2 116.9 %copy-start = (bf16[1,1,18,128,128]{4,3,2,1,0:T(8,128)(2,1)S(1)}, bf16[1,1,18,128,128]{4,3,2,1,0:T(8,128)(2,1)}, u32[]{:S(2)}) copy-start(bf16[1,1,18,128,128]{4,3,2,1,0:T(8,128)(2,1)} %param.12) | copy-start | bytes 1769476
  7.2 188.9 %all-reduce.7.cloned.1.call-start = ((), (), s32[]{:S(2)}) async-start(), calls=%async_computation | async-start | bytes 3145728 | tf_op jit(solution)/shard_map/psum | solution.py:65
  66.7 0.7 copy-start.7
  117.7 2.0 copy-start.2
  199.8 1.0 copy-start.3
  207.2 3.4 copy-start.4
  207.2 3.4 copy-start.6
  216.5 2.9 copy-start.1
  223.3 2.9 copy-start.5
Sparse Core Ops, SparseCore 0:
  128.3 67.7 all-reduce.6
where the time goes:
time: 553 us; the launch traced here: 552 us
  blocking collectives  422 us (76%)
  waiting for transfers between devices  65.9 us (12%)
  matrix products  23.8 us (4%)
  local copies, waits for them, and re-layouts  20.9 us (4%)
  between operations  14.9 us (3%)
    unnamed x1, blocking collectives  316 us
    psum x1, waiting for transfers between devices, per_device(): pre_sum, back_sum = lax.psum((pre_part, back_part), 'wid')  65.9 us
    all_gather x1, blocking collectives, per_device(): lax.all_gather(tokens, 'hid', axis=0, tiled=True)  57.5 us
    all_gather x1, blocking collectives, per_device(): lax.all_gather(out_grad, 'hid', axis=0, tiled=True)  48.8 us
  transfers between devices with their start and end apart: 1, of which 1 were waited for; matrix products, arithmetic and copies ran while one was open for 0% of the time, Pallas kernels for 0%

commit v1 on v0

v1 whole, which is shorter than its diff:
```python
import functools

import jax
import jax.numpy as jnp
from jax import lax
from jax.experimental import pallas as pl
from jax.experimental.pallas import tpu as pltpu
from jax.sharding import PartitionSpec as P

MESH = pl.DeviceIdType.MESH
BF = jnp.bfloat16
F32 = jnp.float32

ROOT = 0.7978845608028654
CUBIC = 0.044715


def gelu_both(v):
    inner = jnp.tanh(ROOT * (v + CUBIC * v * v * v))
    value = 0.5 * v * (1.0 + inner)
    slope = 0.5 * (1.0 + inner) + 0.5 * v * (1.0 - inner * inner) * ROOT * (
        1.0 + 3.0 * CUBIC * v * v
    )
    return value, slope


def kernel(
    x_in, g_in, ut_hbm, dt_hbm, us, ds,
    mixed_out, gt_out, gu_hbm, gd_hbm,
    ut, dt, w1, w2, xcar, gcar, flat, xs, gs, xt, gt, htile, dtile, part, rcore, sb, rx, hd,
    mcar, tcar, msend, mrecv, tsend, trecv, ms2, mr2, ts2, tr2, rows4, gu, gd,
    ssem, rsem, lsem,
):
    hid, wid = lax.axis_index("hid"), lax.axis_index("wid")
    z, y = lax.div(hid, 8), lax.rem(hid, 8)
    xx, c = lax.div(wid, 2), lax.rem(wid, 2)

    def at(zz, yy):
        return (lax.rem(zz + 8, 8) * 8 + lax.rem(yy + 8, 8), wid)

    def up8(v):
        return lax.rem(v + 16, 8)

    xpeer = [(hid, lax.rem(xx + o, 4) * 2 + c) for o in (1, 2, 3)]
    partner = (hid, xx * 2 + 1 - c)

    counter = [0]
    sent = []

    def rcopy(src, dst, dev):
        k = counter[0]
        counter[0] += 1
        cp = pltpu.make_async_remote_copy(
            src_ref=src, dst_ref=dst, send_sem=ssem.at[k], recv_sem=rsem.at[k],
            device_id=dev, device_id_type=MESH,
        )
        cp.start()
        sent.append(cp)
        return cp

    load_ut = pltpu.make_async_copy(ut_hbm.at[0, 0], ut, lsem.at[0])
    load_dt = pltpu.make_async_copy(dt_hbm.at[0, 0], dt, lsem.at[1])
    load_ut.start()
    load_dt.start()

    barrier = pltpu.get_barrier_semaphore()
    peers = [at(z, y + o) for o in range(1, 8)] + [at(z + o, y) for o in range(1, 8)]
    peers += xpeer + [partner]
    for dev in peers:
        pl.semaphore_signal(barrier, inc=1, device_id=dev, device_id_type=MESH)

    def to_rows(src, dst):
        val = src[...].astype(F32)
        for r in range(12):
            rows4[4 * r : 4 * r + 4, :] = val[:, r * 128 : (r + 1) * 128]
        dst[...] = rows4[...].astype(BF)

    to_rows(x_in, xcar.at[z, y])
    to_rows(g_in, gcar.at[y, z])
    pl.semaphore_wait(barrier, len(peers))

    first_x = [rcopy(xcar.at[z, y], xcar.at[z, y], at(z, y + o)) for o in range(1, 8)]
    first_g = [rcopy(gcar.at[y, z], gcar.at[y, z], at(z + o, y)) for o in range(1, 8)]

    load_ut.wait()
    load_dt.wait()

    def build(slots, tiles, dense, rows, cols):
        def one(row, carry):
            for col in range(cols):
                spot = row * cols + col
                below, hits = jnp.int32(0), jnp.int32(0)
                for n in range(18):
                    slot = slots[0, 0, n]
                    below = below + (slot < spot).astype(jnp.int32)
                    hits = hits + (slot == spot).astype(jnp.int32)
                tile = tiles[jnp.minimum(below, 17)]
                dense[
                    pl.ds(pl.multiple_of(row * 128, 128), 128), col * 128 : (col + 1) * 128
                ] = jnp.where(hits > 0, tile, jnp.zeros_like(tile))
            return carry

        lax.fori_loop(0, rows, one, jnp.int32(0))

    for cp in first_x + first_g:
        cp.wait_recv()

    right_x, right_g = at(z + 1, y), at(z, y + 1)
    left_x, left_g = at(z - 1, y), at(z, y - 1)
    for s in range(4):
        step = []
        a, b = up8(z - s), up8(y - s)
        step.append(rcopy(xcar.at[a], xcar.at[a], right_x))
        step.append(rcopy(gcar.at[b], gcar.at[b], right_g))
        if s < 3:
            a, b = up8(z + s), up8(y + s)
            step.append(rcopy(xcar.at[a], xcar.at[a], left_x))
            step.append(rcopy(gcar.at[b], gcar.at[b], left_g))
        if s == 0:
            build(us, ut, w1, 12, 6)
        if s == 1:
            build(ds, dt, w2, 6, 12)
        for cp in step:
            cp.wait_recv()

    def spread(src, dst, tiled, zstep, ystep):
        flat[...] = src[...].reshape(3072, 128).astype(F32)

        def one(zz, carry):
            for r in range(12):
                rows = [
                    flat[pl.ds(zz * zstep + 4 * r + i, 8, stride=ystep), :] for i in range(4)
                ]
                val = jnp.concatenate(rows, axis=0).astype(BF)
                span = pl.ds(pl.multiple_of(zz * 32, 32), 32)
                dst[span, r * 128 : (r + 1) * 128] = val
                tiled[r, span, :] = val
            return carry

        lax.fori_loop(0, 8, one, jnp.int32(0))

    spread(xcar, xs, xt, 384, 48)
    pre = jnp.dot(xs[...], w1[...], preferred_element_type=F32)
    part[0, 0] = pre[:, :384]
    part[1, 0] = pre[:, 384:]
    core_x = rcopy(part.at[1 - c, 0], rcore.at[0], partner)
    spread(gcar, gs, gt, 48, 384)
    back = lax.dot_general(
        gs[...], w2[...], (((1,), (1,)), ((), ())), preferred_element_type=F32
    )
    part[0, 1] = back[:, :384]
    part[1, 1] = back[:, 384:]
    core_g = rcopy(part.at[1 - c, 1], rcore.at[1], partner)

    over = []
    for a, cp in ((0, core_x), (1, core_g)):
        cp.wait_recv()
        total = part[c, a] + rcore[a]
        rcore[a] = total
        sb[a] = total.astype(BF).reshape(4, 64, 384)
        for dev, o in zip(xpeer, (1, 2, 3)):
            over.append(rcopy(sb.at[a, lax.rem(xx + o, 4)], rx.at[a, o], dev))
    sums = []
    for a in range(2):
        acc = rcore[a, pl.ds(pl.multiple_of(xx * 64, 64), 64), :]
        for o in (1, 2, 3):
            over[a * 3 + o - 1].wait_recv()
            acc = acc + rx[a, o].astype(F32)
        sums.append(acc)
    value, slope = gelu_both(sums[0])

    def piece(xv, cv):
        return hd.at[
            :, pl.ds(pl.multiple_of(xv * 64, 64), 64), pl.ds(pl.multiple_of(cv * 384, 128), 384)
        ]

    mine = piece(xx, c)
    mine[0] = value.astype(BF)
    mine[1] = (sums[1] * slope).astype(BF)
    spreadx = [rcopy(mine, mine, dev) for dev in xpeer]
    cross = [rcopy(mine, mine, partner)]
    for cp, o in zip(spreadx, (1, 2, 3)):
        cp.wait_recv()
        got = piece(lax.rem(xx + 4 - o, 4), c)
        cross.append(rcopy(got, got, partner))
    for cp in cross:
        cp.wait_recv()

    def gather_rows(val, r, car, zstep, ystep):
        for zz in range(8):
            for i in range(4):
                car[pl.ds(zz * zstep + 4 * r + i, 8, stride=ystep), :] = val[
                    zz * 32 + i * 8 : zz * 32 + i * 8 + 8, :
                ]

    def mixed_cols(q, carry):
        cols = pl.ds(pl.multiple_of(q * 256, 256), 256)
        val = jnp.dot(hd[0], w2[:, cols], preferred_element_type=F32)
        gather_rows(val[:, :128], 2 * q, mcar, 384, 48)
        gather_rows(val[:, 128:], 2 * q + 1, mcar, 384, 48)
        return carry

    def back_cols(q, carry):
        rows = pl.ds(pl.multiple_of(q * 256, 256), 256)
        val = lax.dot_general(
            hd[1], w1[rows, :], (((1,), (1,)), ((), ())), preferred_element_type=F32
        )
        gather_rows(val[:, :128], 2 * q, tcar, 48, 384)
        gather_rows(val[:, 128:], 2 * q + 1, tcar, 48, 384)
        return carry

    def chunk(car, d):
        return car[pl.ds(pl.multiple_of(d * 384, 384), 384), :]

    def ring_send(car, send, recv, pos, right, left, s, prev):
        out = []
        d = up8(pos + 4 - s)
        val = chunk(car, d)
        if s > 0:
            prev[0].wait_recv()
            val = val + recv[0, s - 1].astype(F32)
        send[0, s] = val.astype(BF)
        out.append(rcopy(send.at[0, s], recv.at[0, s], right))
        if s < 3:
            d = up8(pos - 3 + s)
            val = chunk(car, d)
            if s > 0:
                prev[1].wait_recv()
                val = val + recv[1, s - 1].astype(F32)
            send[1, s] = val.astype(BF)
            out.append(rcopy(send.at[1, s], recv.at[1, s], left))
        else:
            out.append(prev[1])
        return out

    lax.fori_loop(0, 6, mixed_cols, jnp.int32(0))
    m_prev = ring_send(mcar, msend, mrecv, z, right_x, left_x, 0, None)
    lax.fori_loop(0, 6, back_cols, jnp.int32(0))
    t_prev = ring_send(tcar, tsend, trecv, y, right_g, left_g, 0, None)

    def one_up(n, carry):
        slot = us[0, 0, n]
        r, b = lax.div(slot, 6), lax.rem(slot, 6)
        lhs, rhs = xt[r], dtile[b]
        gu[n] = lax.dot_general(lhs, rhs, (((0,), (0,)), ((), ())), preferred_element_type=F32)
        return carry

    def one_down(n, carry):
        slot = ds[0, 0, n]
        b, r = lax.div(slot, 12), lax.rem(slot, 12)
        lhs, rhs = htile[b], gt[r]
        gd[n] = lax.dot_general(lhs, rhs, (((0,), (0,)), ((), ())), preferred_element_type=F32)
        return carry

    for b in range(6):
        htile[b] = hd[0, :, b * 128 : (b + 1) * 128]
        dtile[b] = hd[1, :, b * 128 : (b + 1) * 128]

    stores = []
    for s in (1, 2, 3):
        if s == 1:
            lax.fori_loop(0, 18, one_up, jnp.int32(0))
            stores.append(pltpu.make_async_copy(gu, gu_hbm.at[0, 0], lsem.at[2]))
            stores[-1].start()
        if s == 2:
            lax.fori_loop(0, 18, one_down, jnp.int32(0))
            stores.append(pltpu.make_async_copy(gd, gd_hbm.at[0, 0], lsem.at[3]))
            stores[-1].start()
        m_prev = ring_send(mcar, msend, mrecv, z, right_x, left_x, s, m_prev)
        t_prev = ring_send(tcar, tsend, trecv, y, right_g, left_g, s, t_prev)

    def finish_ring(car, recv, pos, prev, send2):
        prev[0].wait_recv()
        prev[1].wait_recv()
        val = chunk(car, pos) + recv[0, 3].astype(F32) + recv[1, 2].astype(F32)
        car[pl.ds(pl.multiple_of(pos * 384, 384), 384), :] = val
        send2[...] = val.astype(BF).reshape(8, 48, 128)

    finish_ring(mcar, mrecv, z, m_prev, ms2)
    last_m = [rcopy(ms2.at[up8(y + o)], mr2.at[o], at(z, y + o)) for o in range(1, 8)]
    finish_ring(tcar, trecv, y, t_prev, ts2)
    last_t = [rcopy(ts2.at[up8(z + o)], tr2.at[o], at(z + o, y)) for o in range(1, 8)]

    def finish(car, base, recv2, last, out):
        acc = car[pl.ds(pl.multiple_of(base, 48), 48), :]
        for o in range(1, 8):
            last[o - 1].wait_recv()
            acc = acc + recv2[o].astype(F32)
        rows4[...] = acc
        cols = [rows4[4 * r : 4 * r + 4, :] for r in range(12)]
        out[...] = jnp.concatenate(cols, axis=1).astype(BF)

    finish(mcar, z * 384 + y * 48, mr2, last_m, mixed_out)
    finish(tcar, y * 384 + z * 48, tr2, last_t, gt_out)

    for cp in sent:
        cp.wait_send()
    for cp in stores:
        cp.wait()


N_COPIES = 14 + 14 + 2 + 6 + 3 + 4 + 14 + 14


def per_device(tokens, out_grad, up_tiles, down_tiles, up_slots, down_slots):
    vmem = pl.BlockSpec(memory_space=pltpu.VMEM)
    smem = pl.BlockSpec(memory_space=pltpu.SMEM)
    hbm = pl.BlockSpec(memory_space=pl.ANY)
    V = pltpu.VMEM
    return pl.pallas_call(
        kernel,
        out_shape=(
            jax.ShapeDtypeStruct((4, 1536), BF),
            jax.ShapeDtypeStruct((4, 1536), BF),
            jax.ShapeDtypeStruct((1, 1, 18, 128, 128), F32),
            jax.ShapeDtypeStruct((1, 1, 18, 128, 128), F32),
        ),
        in_specs=[vmem, vmem, hbm, hbm, smem, smem],
        out_specs=(vmem, vmem, hbm, hbm),
        scratch_shapes=[
            V((18, 128, 128), BF),
            V((18, 128, 128), BF),
            V((1536, 768), BF),
            V((768, 1536), BF),
            V((8, 8, 48, 128), BF),
            V((8, 8, 48, 128), BF),
            V((3072, 128), F32),
            V((256, 1536), BF),
            V((256, 1536), BF),
            V((12, 256, 128), BF),
            V((12, 256, 128), BF),
            V((6, 256, 128), BF),
            V((6, 256, 128), BF),
            V((2, 2, 256, 384), F32),
            V((2, 256, 384), F32),
            V((2, 4, 64, 384), BF),
            V((2, 4, 64, 384), BF),
            V((2, 256, 768), BF),
            V((3072, 128), F32),
            V((3072, 128), F32),
            V((2, 4, 384, 128), BF),
            V((2, 4, 384, 128), BF),
            V((2, 4, 384, 128), BF),
            V((2, 4, 384, 128), BF),
            V((8, 48, 128), BF),
            V((8, 48, 128), BF),
            V((8, 48, 128), BF),
            V((8, 48, 128), BF),
            V((48, 128), F32),
            V((18, 128, 128), F32),
            V((18, 128, 128), F32),
            pltpu.SemaphoreType.DMA((N_COPIES,)),
            pltpu.SemaphoreType.DMA((N_COPIES,)),
            pltpu.SemaphoreType.DMA((4,)),
        ],
        compiler_params=pltpu.CompilerParams(
            collective_id=0, has_side_effects=True, vmem_limit_bytes=48 * 1024 * 1024
        ),
    )(tokens, out_grad, up_tiles, down_tiles, up_slots, down_slots)


def solution(mesh):
    spec2, spec5, spec3 = P("hid", "wid"), P("hid", "wid", None, None, None), P("hid", "wid", None)
    return jax.shard_map(
        per_device,
        mesh=mesh,
        in_specs=(spec2, spec2, spec5, spec5, spec3, spec3),
        out_specs=(spec2, spec2, spec5, spec5),
        check_vma=False,
    )
```

time: 553 us -> 94.3 us (0.17)
  blocking collectives: 422 us -> 0 us
  Pallas kernels: 0 us -> 85 us
  waiting for transfers between devices: 65.9 us -> 0 us
  matrix products: 23.8 us -> 0 us
  between operations: 14.9 us -> 0.66 us
  local copies, waits for them, and re-layouts: 20.9 us -> 8.07 us
    unnamed x1 -> x0, blocking collectives: 316 us -> none
    all_gather x2 -> x0, blocking collectives: 106 us -> none  [the longest x1 57.5 us: per_device(): lax.all_gather(tokens, 'hid', axis=0, tiled=True)]
    pallas_call x0 -> x1, Pallas kernels: none -> 85 us  [per_device(): pl.pallas_call(kernel, out_shape=(jax.ShapeDtypeStruct((4, 1536), BF), ja...]
    psum x1 -> x0, waiting for transfers between devices: 65.9 us -> none  [per_device(): pre_sum, back_sum = lax.psum((pre_part, back_part), 'wid')]
    dot_general x10 -> x0, matrix products: 23.8 us -> none  [the longest x1 3.85 us: per_device(): jnp.einsum('tnj,nc->tcj', product, col_hot, precision=highest)]
    transpose x4 -> x0, local copies, waits for them, and re-layouts: 8.2 us -> none  [the longest x1 2.93 us: per_device(): jnp.einsum('tnk,nr->trk', product, row_hot, precision=highest)]
  transfers between devices with their start and end apart: 1 -> 0, of which waited for: 1 -> 0; matrix products, arithmetic and copies ran while one was open for 0% -> 0% of each run, Pallas kernels for 0% -> 0%
where the time goes in v1:
time: 94.3 us; the launch traced here: 93.7 us
  Pallas kernels  85 us (90%)
  local copies, waits for them, and re-layouts  8.07 us (9%)
    pallas_call x1, Pallas kernels, per_device(): pl.pallas_call(kernel, out_shape=(jax.ShapeDtypeStruct((4, 1536), BF), ja...  85 us
    unnamed x16, local copies, waits for them, and re-layouts  8.07 us

profile of v1, /device:TPU:6, one launch (start us, length us, event | category | flops | bytes accessed | tf_op | source)
XLA Modules:
  0.0 93.7 jit_solution(6250787150382781055)
XLA Ops:
  0.6 0.0 copy-start
  0.6 1.1 %copy-done = bf16[1,1,18,128,128]{4,3,2,1,0:T(8,128)(2,1)S(1)} copy-done((bf16[1,1,18,128,128]{4,3,2,1,0:T(8,128)(2,1)S(1)}, bf16[1,1,18,128,128]{4,3,2,1,0:T(8,128)(2,1)}, u32[]{:S(2)}) %copy-start) | copy-done | bytes 589848
  1.7 0.0 copy-start.1
  1.7 1.1 %copy-done.1 = bf16[1,1,18,128,128]{4,3,2,1,0:T(8,128)(2,1)S(1)} copy-done((bf16[1,1,18,128,128]{4,3,2,1,0:T(8,128)(2,1)S(1)}, bf16[1,1,18,128,128]{4,3,2,1,0:T(8,128)(2,1)}, u32[]{:S(2)}) %copy-start.1) | copy-done | bytes 589848
  2.8 0.0 copy-start.2
  2.8 0.7 copy-done.2
  3.5 0.0 copy-start.3
  3.5 0.7 copy-done.3
  4.2 0.0 copy-start.4
  4.2 0.7 copy-done.4
  4.8 0.0 copy-start.5
  4.8 0.7 copy-done.5
  5.5 85.0 %shard_map.93 = (bf16[4,1536]{1,0:T(4,128)(2,1)S(1)}, bf16[4,1536]{1,0:T(4,128)(2,1)S(1)}, f32[1,1,18,128,128]{4,3,2,1,0:T(8,128)S(1)}, f32[1,1,18,128,128]{4,3,2,1,0:T(8,128)S(1)}) custom-call(bf16[4,1536]{1,0:T(4,128)(2,1)S(1)} %copy-done.2, bf16[4,1536]{1,0:T(4,128)(2,1)S(1)} %copy-done.3, bf16[1,1,18,128,128]{4,3,2,1,0:T(8,128)(2,1)S(1)} %copy-done, ...), custom_call_target="tpu_custom_call" | custom-call | tf_op jit(solution)/shard_map/pallas_call | solution.py:310
  90.5 0.6 copy.14
  91.1 0.6 copy.15
  91.7 1.0 %copy.16 = f32[1,1,18,128,128]{4,3,2,1,0:T(8,128)} copy(f32[1,1,18,128,128]{4,3,2,1,0:T(8,128)S(1)} %get-tuple-element.10) | data formatting | bytes 2359296
  92.7 1.0 %copy.17 = f32[1,1,18,128,128]{4,3,2,1,0:T(8,128)} copy(f32[1,1,18,128,128]{4,3,2,1,0:T(8,128)S(1)} %get-tuple-element.11) | data formatting | bytes 2359296
Async XLA Ops:
  0.6 1.1 %copy-start = (bf16[1,1,18,128,128]{4,3,2,1,0:T(8,128)(2,1)S(1)}, bf16[1,1,18,128,128]{4,3,2,1,0:T(8,128)(2,1)}, u32[]{:S(2)}) copy-start(bf16[1,1,18,128,128]{4,3,2,1,0:T(8,128)(2,1)} %ut_hbm.1) | copy-start | bytes 1769476
  1.7 1.1 %copy-start.1 = (bf16[1,1,18,128,128]{4,3,2,1,0:T(8,128)(2,1)S(1)}, bf16[1,1,18,128,128]{4,3,2,1,0:T(8,128)(2,1)}, u32[]{:S(2)}) copy-start(bf16[1,1,18,128,128]{4,3,2,1,0:T(8,128)(2,1)} %dt_hbm.1) | copy-start | bytes 1769476
  2.8 0.7 copy-start.2
  3.5 0.7 copy-start.3
  4.2 0.7 copy-start.4
  4.8 0.7 copy-start.5

commit v2 on v1

v2 whole, which is shorter than its diff:
```python
import jax
import jax.numpy as jnp
from jax import lax
from jax.experimental import pallas as pl
from jax.experimental.pallas import tpu as pltpu
from jax.sharding import PartitionSpec as P

MESH = pl.DeviceIdType.MESH
BF = jnp.bfloat16
F32 = jnp.float32

ROOT = 0.7978845608028654
CUBIC = 0.044715

NEAR = (0, 1, 3, 2)
FAR = (2, 3, 1, 0)


def gelu_both(v):
    inner = jnp.tanh(ROOT * (v + CUBIC * v * v * v))
    value = 0.5 * v * (1.0 + inner)
    slope = 0.5 * (1.0 + inner) + 0.5 * v * (1.0 - inner * inner) * ROOT * (
        1.0 + 3.0 * CUBIC * v * v
    )
    return value, slope


def up8(v):
    return lax.rem(v + 16, 8)


def drain(sent, stores):
    for cp in sent:
        cp.wait_send()
    for cp in stores:
        cp.wait()


def kernel(
    x_hbm, g_hbm, ut_hbm, dt_hbm, us_hbm, ds_hbm,
    mixed_out, gt_out, gu_hbm, gd_hbm,
    x_in, g_in, us, ds, ut, dt, w1, w2, xcar, gcar, xflat, gflat, xs, gs, xt, gt,
    part, rcore, sb, rx, hb, db, slopes, backs, htile, dtile,
    mcar, tcar, msend, mrecv, tsend, trecv, ms2, mr2, ts2, tr2, rows4, gu, gd,
    ssem, rsem, lsem,
):
    hid, wid = lax.axis_index("hid"), lax.axis_index("wid")
    z, y = lax.div(hid, 8), lax.rem(hid, 8)
    xx, c = lax.div(wid, 2), lax.rem(wid, 2)

    def at(zz, yy):
        return (up8(zz) * 8 + up8(yy), wid)

    def pair(pos, k):
        q = lax.div(pos, 2)
        return (q, q + 1 - 2 * lax.rem(q, 2), lax.rem(q + 2, 4), 3 - q)[k]

    def mate(pos, k, b):
        low = lax.rem(pos, 2)
        return pair(pos, k) * 2 + (1 - low if b else low)

    others = [(k, b) for k in NEAR for b in (0, 1) if (k, b) != (0, 0)]
    xpeer = [(hid, lax.rem(xx + o, 4) * 2 + c) for o in (1, 2, 3)]
    partner = (hid, xx * 2 + 1 - c)

    counter = [0]
    sent = []
    stores = []

    def rcopy(src, dst, dev):
        k = counter[0]
        counter[0] += 1
        cp = pltpu.make_async_remote_copy(
            src_ref=src, dst_ref=dst, send_sem=ssem.at[k], recv_sem=rsem.at[k],
            device_id=dev, device_id_type=MESH,
        )
        cp.start()
        sent.append(cp)
        return cp

    loads = [
        pltpu.make_async_copy(a, b, lsem.at[n])
        for n, (a, b) in enumerate(
            (
                (x_hbm, x_in), (g_hbm, g_in), (us_hbm, us), (ds_hbm, ds),
                (ut_hbm.at[0, 0], ut), (dt_hbm.at[0, 0], dt),
            )
        )
    ]
    for cp in loads:
        cp.start()

    barrier = pltpu.get_barrier_semaphore()
    peers = [at(z, mate(y, k, b)) for k, b in others] + [at(mate(z, k, b), y) for k, b in others]
    peers += xpeer + [partner]
    for dev in peers:
        pl.semaphore_signal(barrier, inc=1, device_id=dev, device_id_type=MESH)

    def to_rows(src, dst):
        val = src[...].astype(F32)
        for r in range(12):
            rows4[4 * r : 4 * r + 4, :] = val[:, r * 128 : (r + 1) * 128]
        dst[...] = rows4[...].astype(BF)

    loads[0].wait()
    to_rows(x_in, xcar.at[z, y])
    loads[1].wait()
    to_rows(g_in, gcar.at[y, z])
    pl.semaphore_wait(barrier, len(peers))

    first = {}
    for k, b in others:
        first["x", k, b] = rcopy(xcar.at[z, y], xcar.at[z, y], at(z, mate(y, k, b)))
        first["g", k, b] = rcopy(gcar.at[y, z], gcar.at[y, z], at(mate(z, k, b), y))

    for cp in loads[2:]:
        cp.wait()

    def build(slots, tiles, dense, rows, cols):
        def one(row, carry):
            pos = jnp.int32(0)
            for n in range(18):
                pos = pos + (slots[0, 0, n] < row * cols).astype(jnp.int32)
            for col in range(cols):
                idx = jnp.minimum(pos, 17)
                hit = jnp.logical_and(pos < 18, slots[0, 0, idx] == row * cols + col)
                tile = tiles[idx]
                dense[
                    pl.ds(pl.multiple_of(row * 128, 128), 128), col * 128 : (col + 1) * 128
                ] = jnp.where(hit, tile, jnp.zeros_like(tile))
                pos = pos + hit.astype(jnp.int32)
            return carry

        lax.fori_loop(0, rows, one, jnp.int32(0))

    build(us, ut, w1, 12, 6)
    build(ds, dt, w2, 6, 12)

    axes = {
        "x": (xcar, z, y, at(z + 1, y), at(z - 1, y)),
        "g": (gcar, y, z, at(z, y + 1), at(z, y - 1)),
    }
    ring = {}

    def offsets(g):
        return (-g, g + 1)

    def step(s):
        for k in NEAR:
            for name in ("x", "g"):
                car, pos, cross, right, left = axes[name]
                if s == 0:
                    for b in (0, 1):
                        if (k, b) != (0, 0):
                            first[name, k, b].wait_recv()
                else:
                    ring[name, s - 1, k, "r"].wait_recv()
                    if s < 4:
                        ring[name, s - 1, k, "l"].wait_recv()
                span = pl.ds(pair(cross, k) * 2, 2)
                if s < 4:
                    ref = car.at[up8(pos - s), span]
                    ring[name, s, k, "r"] = rcopy(ref, ref, right)
                if s < 3:
                    ref = car.at[up8(pos + s), span]
                    ring[name, s, k, "l"] = rcopy(ref, ref, left)

    def unpack(car, pos, flat, dst, g):
        for off in offsets(g):
            d = up8(pos + off)
            flat[pl.ds(pl.multiple_of(d * 384, 384), 384), :] = (
                car[d].reshape(384, 128).astype(F32)
            )

        def cols(t, carry):
            for u in range(2):
                r = 2 * t + u
                for i in range(4):
                    rows = [
                        flat[pl.ds(up8(pos + off) * 384 + 4 * r + i, 8, stride=48), :]
                        for off in offsets(g)
                    ]
                    dst[g, i * 16 : (i + 1) * 16, pl.ds(pl.multiple_of(r * 128, 128), 128)] = (
                        jnp.concatenate(rows, axis=0).astype(BF)
                    )
            return carry

        lax.fori_loop(0, 6, cols, jnp.int32(0))

    core = {}
    over = {}
    back_home = {}

    def halves(val, g, a):
        part[g, 0, a] = val[:, :384]
        part[g, 1, a] = val[:, 384:]
        core[g, a] = rcopy(part.at[g, 1 - c, a], rcore.at[g, a], partner)

    def compute_x(g):
        unpack(xcar, z, xflat, xs, g)
        halves(jnp.dot(xs[g], w1[...], preferred_element_type=F32), g, 0)

    def compute_g(g):
        unpack(gcar, y, gflat, gs, g)
        halves(
            lax.dot_general(
                gs[g], w2[...], (((1,), (1,)), ((), ())), preferred_element_type=F32
            ),
            g,
            1,
        )

    def sum_cores(g):
        for a in range(2):
            core[g, a].wait_recv()
            total = part[g, c, a] + rcore[g, a]
            rcore[g, a] = total
            for i in range(4):
                sb[g, i, a] = total[i * 16 : (i + 1) * 16].astype(BF)
        for dev, o in zip(xpeer, (1, 2, 3)):
            over[g, o] = rcopy(sb.at[g, lax.rem(xx + o, 4)], rx.at[g, o], dev)

    def mine(buf, g, i):
        return buf.at[
            g,
            pl.ds(pl.multiple_of(i * 16, 16), 16),
            pl.ds(pl.multiple_of(c * 384, 128), 384),
        ]

    def send_home(buf, name, g):
        ref = mine(buf, g, xx)
        back_home[name, g] = [rcopy(ref, ref, dev) for dev in xpeer] + [rcopy(ref, ref, partner)]

    def relay(buf, name, g):
        for n, o in enumerate((1, 2, 3)):
            back_home[name, g][n].wait_recv()
            ref = mine(buf, g, lax.rem(xx + 4 - o, 4))
            back_home[name, g].append(rcopy(ref, ref, partner))

    def all_home(name, g):
        for cp in back_home[name, g][3:]:
            cp.wait_recv()

    def sum_chips(g):
        acc = [rcore[g, a, pl.ds(pl.multiple_of(xx * 16, 16), 16), :] for a in range(2)]
        for o in (1, 2, 3):
            over[g, o].wait_recv()
            acc = [acc[a] + rx[g, o, a].astype(F32) for a in range(2)]
        value, slope = gelu_both(acc[0])
        ref = mine(hb, g, xx)
        ref[...] = value.astype(BF)
        send_home(hb, "h", g)
        for n, off in enumerate(offsets(g)):
            dz, dy = up8(z + off), up8(y + off)
            for t in range(3):
                lanes = slice(t * 128, (t + 1) * 128)
                slopes[t, pl.ds(pl.multiple_of(dz * 8, 8), 8), :] = slope[
                    n * 8 : (n + 1) * 8, lanes
                ]
                backs[t, pl.ds(pl.multiple_of(dy * 8, 8), 8), :] = acc[1][
                    n * 8 : (n + 1) * 8, lanes
                ]

    def delta(g):
        rows = []
        for off in offsets(g):
            dy = up8(y + off)
            rows.append(
                jnp.concatenate(
                    [
                        backs[t, pl.ds(pl.multiple_of(dy * 8, 8), 8), :]
                        * slopes[t, pl.ds(dy, 8, stride=8), :]
                        for t in range(3)
                    ],
                    axis=1,
                )
            )
        ref = mine(db, g, xx)
        ref[...] = jnp.concatenate(rows, axis=0).astype(BF)
        send_home(db, "d", g)

    def retile(flat, pos, dst):
        def one(g, carry):
            for r in range(12):
                for i in range(4):
                    rows = [
                        flat[pl.ds(up8(pos - g + n * (2 * g + 1)) * 48 + 4 * r + i, 8, stride=384), :]
                        for n in range(2)
                    ]
                    dst[r, pl.ds(pl.multiple_of(g * 64 + i * 16, 16), 16), :] = jnp.concatenate(
                        rows, axis=0
                    ).astype(BF)
            return carry

        lax.fori_loop(0, 4, one, jnp.int32(0))

    def pack(val, r, car, pos, groups):
        for n, g in enumerate(groups):
            for i in range(4):
                for m, off in enumerate(offsets(g)):
                    lo = n * 64 + i * 16 + m * 8
                    car[pl.ds(up8(pos + off) * 384 + 4 * r + i, 8, stride=48), :] = val[lo : lo + 8]

    def mixed_part(groups):
        lhs = jnp.concatenate([hb[g] for g in groups], axis=0)

        def cols(q, carry):
            val = jnp.dot(
                lhs, w2[:, pl.ds(pl.multiple_of(q * 256, 256), 256)], preferred_element_type=F32
            )
            pack(val[:, :128], 2 * q, mcar, z, groups)
            pack(val[:, 128:], 2 * q + 1, mcar, z, groups)
            return carry

        lax.fori_loop(0, 6, cols, jnp.int32(0))

    def back_part(groups):
        lhs = jnp.concatenate([db[g] for g in groups], axis=0)

        def cols(q, carry):
            val = lax.dot_general(
                lhs,
                w1[pl.ds(pl.multiple_of(q * 256, 256), 256), :],
                (((1,), (1,)), ((), ())),
                preferred_element_type=F32,
            )
            pack(val[:, :128], 2 * q, tcar, y, groups)
            pack(val[:, 128:], 2 * q + 1, tcar, y, groups)
            return carry

        lax.fori_loop(0, 6, cols, jnp.int32(0))

    outs = {
        "m": (mcar, msend, mrecv, z, y, at(z + 1, y), at(z - 1, y)),
        "t": (tcar, tsend, trecv, y, z, at(z, y + 1), at(z, y - 1)),
    }
    rsum = {}

    def ring_send(name, s):
        car, send, recv, pos, cross, right, left = outs[name]
        for k in FAR:
            at_rows = pair(cross, k) * 96
            span = pl.ds(pl.multiple_of(at_rows, 96), 96)
            for w, dev, d in ((0, right, pos + 4 - s), (1, left, pos - 3 + s)):
                if w == 1 and s == 3:
                    continue
                val = car[pl.ds(pl.multiple_of(up8(d) * 384 + at_rows, 96), 96), :]
                if s > 0:
                    rsum[name, s - 1, k, w].wait_recv()
                    val = val + recv[w, s - 1, span, :].astype(F32)
                send[w, s, span, :] = val.astype(BF)
                rsum[name, s, k, w] = rcopy(
                    send.at[w, s, span, :], recv.at[w, s, span, :], dev
                )

    last = {}

    def ring_end(name, send2, recv2):
        car, send, recv, pos, cross, right, left = outs[name]
        for k in FAR:
            at_rows = pair(cross, k) * 96
            span = pl.ds(pl.multiple_of(at_rows, 96), 96)
            rsum[name, 3, k, 0].wait_recv()
            rsum[name, 2, k, 1].wait_recv()
            here = pl.ds(pl.multiple_of(pos * 384 + at_rows, 96), 96)
            val = car[here, :] + recv[0, 3, span, :].astype(F32) + recv[1, 2, span, :].astype(F32)
            car[here, :] = val
            send2[span, :] = val.astype(BF)
            for b in (0, 1):
                if (k, b) == (0, 0):
                    continue
                to = mate(cross, k, b)
                dev = at(pos, to) if name == "m" else at(to, pos)
                n = 2 * k + b
                last[name, k, b] = rcopy(
                    send2.at[pl.ds(pl.multiple_of(to * 48, 48), 48), :], recv2.at[n], dev
                )

    def one_up(n, carry):
        slot = us[0, 0, n]
        lhs, rhs = xt[lax.div(slot, 6)], dtile[lax.rem(slot, 6)]
        gu[n] = lax.dot_general(lhs, rhs, (((0,), (0,)), ((), ())), preferred_element_type=F32)
        return carry

    def one_down(n, carry):
        slot = ds[0, 0, n]
        lhs, rhs = htile[lax.div(slot, 12)], gt[lax.rem(slot, 12)]
        gd[n] = lax.dot_general(lhs, rhs, (((0,), (0,)), ((), ())), preferred_element_type=F32)
        return carry

    def tile_up(buf, dst):
        for b in range(6):
            dst[b] = buf[:, :, b * 128 : (b + 1) * 128].reshape(256, 128)

    def store(src, dst, n):
        stores.append(pltpu.make_async_copy(src, dst.at[0, 0], lsem.at[n]))
        stores[-1].start()

    step(0)
    step(1)
    compute_x(0)
    compute_g(0)
    step(2)
    sum_cores(0)
    compute_x(1)
    compute_g(1)
    step(3)
    sum_chips(0)
    sum_cores(1)
    compute_x(2)
    compute_g(2)
    step(4)
    compute_x(3)
    compute_g(3)
    sum_cores(2)
    sum_chips(1)
    sum_cores(3)
    relay(hb, "h", 0)
    retile(xflat, y, xt)
    sum_chips(2)
    relay(hb, "h", 1)
    sum_chips(3)
    delta(3)
    for g in (2, 1, 0):
        delta(g)
    relay(hb, "h", 2)
    for g in (0, 1, 2):
        all_home("h", g)
    mixed_part((0, 1, 2))
    relay(hb, "h", 3)
    relay(db, "d", 3)
    all_home("h", 3)
    mixed_part((3,))
    ring_send("m", 0)
    all_home("d", 3)
    back_part((3,))
    ring_send("t", 0)
    for g in (2, 1, 0):
        relay(db, "d", g)
    for g in (2, 1, 0):
        all_home("d", g)
    back_part((2, 1, 0))
    ring_send("m", 1)
    ring_send("t", 1)
    tile_up(db, dtile)
    lax.fori_loop(0, 18, one_up, jnp.int32(0))
    store(gu, gu_hbm, 6)
    ring_send("m", 2)
    ring_send("t", 2)
    tile_up(hb, htile)
    retile(gflat, z, gt)
    ring_send("m", 3)
    ring_send("t", 3)
    lax.fori_loop(0, 18, one_down, jnp.int32(0))
    store(gd, gd_hbm, 7)
    ring_end("m", ms2, mr2)
    ring_end("t", ts2, tr2)

    def finish(name, recv2, out):
        car, _, _, pos, cross, _, _ = outs[name]
        acc = car[pl.ds(pl.multiple_of(pos * 384 + cross * 48, 48), 48), :]
        for k, b in others:
            last[name, k, b].wait_recv()
            acc = acc + recv2[2 * k + b].astype(F32)
        rows4[...] = acc
        cols = [rows4[4 * r : 4 * r + 4, :] for r in range(12)]
        out[...] = jnp.concatenate(cols, axis=1).astype(BF)

    finish("m", mr2, mixed_out)
    finish("t", tr2, gt_out)
    drain(sent, stores)


N_COPIES = 14 + 56 + 8 + 12 + 56 + 56 + 14


def per_device(tokens, out_grad, up_tiles, down_tiles, up_slots, down_slots):
    vmem = pl.BlockSpec(memory_space=pltpu.VMEM)
    hbm = pl.BlockSpec(memory_space=pltpu.HBM)
    V = pltpu.VMEM
    return pl.pallas_call(
        kernel,
        out_shape=(
            jax.ShapeDtypeStruct((4, 1536), BF),
            jax.ShapeDtypeStruct((4, 1536), BF),
            jax.ShapeDtypeStruct((1, 1, 18, 128, 128), F32),
            jax.ShapeDtypeStruct((1, 1, 18, 128, 128), F32),
        ),
        in_specs=[hbm] * 6,
        out_specs=(vmem, vmem, hbm, hbm),
        scratch_shapes=[
            V((4, 1536), BF),
            V((4, 1536), BF),
            pltpu.SMEM((1, 1, 18), jnp.int32),
            pltpu.SMEM((1, 1, 18), jnp.int32),
            V((18, 128, 128), BF),
            V((18, 128, 128), BF),
            V((1536, 768), BF),
            V((768, 1536), BF),
            V((8, 8, 48, 128), BF),
            V((8, 8, 48, 128), BF),
            V((3072, 128), F32),
            V((3072, 128), F32),
            V((4, 64, 1536), BF),
            V((4, 64, 1536), BF),
            V((12, 256, 128), BF),
            V((12, 256, 128), BF),
            V((4, 2, 2, 64, 384), F32),
            V((4, 2, 64, 384), F32),
            V((4, 4, 2, 16, 384), BF),
            V((4, 4, 2, 16, 384), BF),
            V((4, 64, 768), BF),
            V((4, 64, 768), BF),
            V((3, 64, 128), F32),
            V((3, 64, 128), F32),
            V((6, 256, 128), BF),
            V((6, 256, 128), BF),
            V((3072, 128), F32),
            V((3072, 128), F32),
            V((2, 4, 384, 128), BF),
            V((2, 4, 384, 128), BF),
            V((2, 4, 384, 128), BF),
            V((2, 4, 384, 128), BF),
            V((384, 128), BF),
            V((8, 48, 128), BF),
            V((384, 128), BF),
            V((8, 48, 128), BF),
            V((48, 128), F32),
            V((18, 128, 128), F32),
            V((18, 128, 128), F32),
            pltpu.SemaphoreType.DMA((N_COPIES,)),
            pltpu.SemaphoreType.DMA((N_COPIES,)),
            pltpu.SemaphoreType.DMA((8,)),
        ],
        compiler_params=pltpu.CompilerParams(
            collective_id=0, has_side_effects=True, vmem_limit_bytes=56 * 1024 * 1024
        ),
    )(tokens, out_grad, up_tiles, down_tiles, up_slots, down_slots)


def solution(mesh):
    spec2, spec5, spec3 = P("hid", "wid"), P("hid", "wid", None, None, None), P("hid", "wid", None)
    return jax.shard_map(
        per_device,
        mesh=mesh,
        in_specs=(spec2, spec2, spec5, spec5, spec3, spec3),
        out_specs=(spec2, spec2, spec5, spec5),
        check_vma=False,
    )
```

time: 94.3 us -> 83.2 us (0.88)
  Pallas kernels: 85 us -> 75.9 us
  local copies, waits for them, and re-layouts: 8.07 us -> 6.12 us
    pallas_call x1, Pallas kernels: 85 us -> 75.9 us  [per_device(): pl.pallas_call(kernel, out_shape=(jax.ShapeDtypeStruct((4, 1536), BF), ja...]
    unnamed x16 -> x6, local copies, waits for them, and re-layouts: 8.07 us -> 6.12 us
where the time goes in v2:
time: 83.2 us; the launch traced here: 82.6 us
  Pallas kernels  75.9 us (91%)
  local copies, waits for them, and re-layouts  6.12 us (7%)
    pallas_call x1, Pallas kernels, per_device(): pl.pallas_call(kernel, out_shape=(jax.ShapeDtypeStruct((4, 1536), BF), ja...  75.9 us
    unnamed x6, local copies, waits for them, and re-layouts  6.12 us

profile of v2, /device:TPU:6, one launch (start us, length us, event | category | flops | bytes accessed | tf_op | source)
XLA Modules:
  0.0 82.6 jit_solution(13162037921824000353)
XLA Ops:
  0.6 75.9 %shard_map.93 = (bf16[4,1536]{1,0:T(4,128)(2,1)}, bf16[4,1536]{1,0:T(4,128)(2,1)}, f32[1,1,18,128,128]{4,3,2,1,0:T(8,128)}, f32[1,1,18,128,128]{4,3,2,1,0:T(8,128)}) custom-call(bf16[4,1536]{1,0:T(4,128)(2,1)} %x_hbm.1, bf16[4,1536]{1,0:T(4,128)(2,1)} %g_hbm.1, bf16[1,1,18,128,128]{4,3,2,1,0:T(8,128)(2,1)} %ut_hbm.1, bf16[1,1,18,128,128]{4,3,2,1,0:T(8,128)(2,1)} %dt_hbm.1, ...), custom_call_target="tpu_custom_call" | custom-call | tf_op jit(solution)/shard_map/pallas_call | solution.py:481
  76.5 1.3 %copy.14 = bf16[4,1536]{1,0:T(4,128)(2,1)} copy(bf16[4,1536]{1,0:T(4,128)(2,1)} %get-tuple-element.8) | data formatting | bytes 24576
  77.8 1.3 %copy.15 = bf16[4,1536]{1,0:T(4,128)(2,1)} copy(bf16[4,1536]{1,0:T(4,128)(2,1)} %get-tuple-element.9) | data formatting | bytes 24576
  79.1 0.0 copy-start
  79.1 2.5 %copy.16 = f32[1,1,18,128,128]{4,3,2,1,0:T(8,128)} copy(f32[1,1,18,128,128]{4,3,2,1,0:T(8,128)} %get-tuple-element.10) | data formatting | bytes 2359296
  81.6 0.0 copy-done
  81.6 1.0 %copy.17 = f32[1,1,18,128,128]{4,3,2,1,0:T(8,128)} copy(f32[1,1,18,128,128]{4,3,2,1,0:T(8,128)S(1)} %copy-done) | data formatting | bytes 2359296
Async XLA Ops:
  79.1 2.5 %copy-start = (f32[1,1,18,128,128]{4,3,2,1,0:T(8,128)S(1)}, f32[1,1,18,128,128]{4,3,2,1,0:T(8,128)}, u32[]{:S(2)}) copy-start(f32[1,1,18,128,128]{4,3,2,1,0:T(8,128)} %get-tuple-element.11) | copy-start | bytes 3538948

commit v3 on v2

--- a/solution.py
+++ b/solution.py
@@ -1,3 +1,5 @@
+import functools
+
 import jax
 import jax.numpy as jnp
 from jax import lax
@@ -36,12 +38,23 @@
         cp.wait()
 
 
+def write_out(a, b, c, d, oa, ob, oc, od, sem):
+    copies = [
+        pltpu.make_async_copy(src, dst, sem.at[n])
+        for n, (src, dst) in enumerate(((a, oa), (b, ob), (c, oc), (d, od)))
+    ]
+    for cp in copies:
+        cp.start()
+    for cp in copies:
+        cp.wait()
+
+
 def kernel(
     x_hbm, g_hbm, ut_hbm, dt_hbm, us_hbm, ds_hbm,
-    mixed_out, gt_out, gu_hbm, gd_hbm,
+    mixed_out, gt_out, gu, gd,
     x_in, g_in, us, ds, ut, dt, w1, w2, xcar, gcar, xflat, gflat, xs, gs, xt, gt,
     part, rcore, sb, rx, hb, db, slopes, backs, htile, dtile,
-    mcar, tcar, msend, mrecv, tsend, trecv, ms2, mr2, ts2, tr2, rows4, gu, gd,
+    mcar, tcar, msend, mrecv, tsend, trecv, ms2, mr2, ts2, tr2, rows4,
     ssem, rsem, lsem,
 ):
     hid, wid = lax.axis_index("hid"), lax.axis_index("wid")
@@ -78,6 +91,12 @@
         sent.append(cp)
         return cp
 
+    barrier = pltpu.get_barrier_semaphore()
+    peers = [at(z, mate(y, k, b)) for k, b in others] + [at(mate(z, k, b), y) for k, b in others]
+    peers += xpeer + [partner]
+    for dev in peers:
+        pl.semaphore_signal(barrier, inc=1, device_id=dev, device_id_type=MESH)
+
     loads = [
         pltpu.make_async_copy(a, b, lsem.at[n])
         for n, (a, b) in enumerate(
@@ -89,12 +108,6 @@
     ]
     for cp in loads:
         cp.start()
-
-    barrier = pltpu.get_barrier_semaphore()
-    peers = [at(z, mate(y, k, b)) for k, b in others] + [at(mate(z, k, b), y) for k, b in others]
-    peers += xpeer + [partner]
-    for dev in peers:
-        pl.semaphore_signal(barrier, inc=1, device_id=dev, device_id_type=MESH)
 
     def to_rows(src, dst):
         val = src[...].astype(F32)
@@ -145,7 +158,14 @@
     def offsets(g):
         return (-g, g + 1)
 
-    def step(s):
+    def run(tasks, share):
+        for _ in range(min(len(tasks), share)):
+            tasks.pop(0)()
+
+    def step(s, tasks=()):
+        tasks = list(tasks)
+        share = -(-len(tasks) // 5)
+        run(tasks, share)
         for k in NEAR:
             for name in ("x", "g"):
                 car, pos, cross, right, left = axes[name]
@@ -164,51 +184,53 @@
                 if s < 3:
                     ref = car.at[up8(pos + s), span]
                     ring[name, s, k, "l"] = rcopy(ref, ref, left)
-
-    def unpack(car, pos, flat, dst, g):
-        for off in offsets(g):
-            d = up8(pos + off)
-            flat[pl.ds(pl.multiple_of(d * 384, 384), 384), :] = (
-                car[d].reshape(384, 128).astype(F32)
-            )
-
-        def cols(t, carry):
-            for u in range(2):
-                r = 2 * t + u
-                for i in range(4):
-                    rows = [
-                        flat[pl.ds(up8(pos + off) * 384 + 4 * r + i, 8, stride=48), :]
-                        for off in offsets(g)
-                    ]
-                    dst[g, i * 16 : (i + 1) * 16, pl.ds(pl.multiple_of(r * 128, 128), 128)] = (
-                        jnp.concatenate(rows, axis=0).astype(BF)
-                    )
-            return carry
-
-        lax.fori_loop(0, 6, cols, jnp.int32(0))
+            run(tasks, share)
+
+    def widen(car, pos, flat, off):
+        d = up8(pos + off)
+        flat[pl.ds(pl.multiple_of(d * 384, 384), 384), :] = car[d].reshape(384, 128).astype(F32)
+
+    def unpack(pos, flat, dst, g, tiles):
+        for r in tiles:
+            for i in range(4):
+                rows = [
+                    flat[pl.ds(up8(pos + off) * 384 + 4 * r + i, 8, stride=48), :]
+                    for off in offsets(g)
+                ]
+                dst[g, i * 16 : (i + 1) * 16, r * 128 : (r + 1) * 128] = jnp.concatenate(
+                    rows, axis=0
+                ).astype(BF)
 
     core = {}
     over = {}
     back_home = {}
 
-    def halves(val, g, a):
-        part[g, 0, a] = val[:, :384]
-        part[g, 1, a] = val[:, 384:]
-        core[g, a] = rcopy(part.at[g, 1 - c, a], rcore.at[g, a], partner)
-
-    def compute_x(g):
-        unpack(xcar, z, xflat, xs, g)
-        halves(jnp.dot(xs[g], w1[...], preferred_element_type=F32), g, 0)
-
-    def compute_g(g):
-        unpack(gcar, y, gflat, gs, g)
-        halves(
-            lax.dot_general(
-                gs[g], w2[...], (((1,), (1,)), ((), ())), preferred_element_type=F32
-            ),
-            g,
-            1,
-        )
+    def product(a, g, q):
+        cols = slice(q * 256, (q + 1) * 256)
+        if a == 0:
+            val = jnp.dot(xs[g], w1[:, cols], preferred_element_type=F32)
+        else:
+            val = lax.dot_general(
+                gs[g], w2[cols, :], (((1,), (1,)), ((), ())), preferred_element_type=F32
+            )
+        for t in range(2):
+            n = 2 * q + t
+            part[g, n // 3, a, :, (n % 3) * 128 : (n % 3 + 1) * 128] = val[
+                :, t * 128 : (t + 1) * 128
+            ]
+        if q == 2:
+            core[g, a] = rcopy(part.at[g, 1 - c, a], rcore.at[g, a], partner)
+
+    def compute(g):
+        tasks = []
+        for a, car, pos, flat, dst in ((0, xcar, z, xflat, xs), (1, gcar, y, gflat, gs)):
+            for off in offsets(g):
+                tasks.append(functools.partial(widen, car, pos, flat, off))
+            for t in range(4):
+                tasks.append(functools.partial(unpack, pos, flat, dst, g, (3 * t, 3 * t + 1, 3 * t + 2)))
+            for q in range(3):
+                tasks.append(functools.partial(product, a, g, q))
+        return tasks
 
     def sum_cores(g):
         for a in range(2):
@@ -376,52 +398,49 @@
                     send2.at[pl.ds(pl.multiple_of(to * 48, 48), 48), :], recv2.at[n], dev
                 )
 
-    def one_up(n, carry):
-        slot = us[0, 0, n]
-        lhs, rhs = xt[lax.div(slot, 6)], dtile[lax.rem(slot, 6)]
-        gu[n] = lax.dot_general(lhs, rhs, (((0,), (0,)), ((), ())), preferred_element_type=F32)
-        return carry
-
-    def one_down(n, carry):
-        slot = ds[0, 0, n]
-        lhs, rhs = htile[lax.div(slot, 12)], gt[lax.rem(slot, 12)]
-        gd[n] = lax.dot_general(lhs, rhs, (((0,), (0,)), ((), ())), preferred_element_type=F32)
-        return carry
+    def up_some(lo, hi):
+        def one(n, carry):
+            slot = us[0, 0, n]
+            lhs, rhs = xt[lax.div(slot, 6)], dtile[lax.rem(slot, 6)]
+            gu[0, 0, n] = lax.dot_general(
+                lhs, rhs, (((0,), (0,)), ((), ())), preferred_element_type=F32
+            )
+            return carry
+
+        lax.fori_loop(lo, hi, one, jnp.int32(0))
+
+    def down_some(lo, hi):
+        def one(n, carry):
+            slot = ds[0, 0, n]
+            lhs, rhs = htile[lax.div(slot, 12)], gt[lax.rem(slot, 12)]
+            gd[0, 0, n] = lax.dot_general(
+                lhs, rhs, (((0,), (0,)), ((), ())), preferred_element_type=F32
+            )
+            return carry
+
+        lax.fori_loop(lo, hi, one, jnp.int32(0))
 
     def tile_up(buf, dst):
         for b in range(6):
             dst[b] = buf[:, :, b * 128 : (b + 1) * 128].reshape(256, 128)
 
-    def store(src, dst, n):
-        stores.append(pltpu.make_async_copy(src, dst.at[0, 0], lsem.at[n]))
-        stores[-1].start()
-
+    P_ = functools.partial
     step(0)
     step(1)
-    compute_x(0)
-    compute_g(0)
-    step(2)
-    sum_cores(0)
-    compute_x(1)
-    compute_g(1)
-    step(3)
-    sum_chips(0)
-    sum_cores(1)
-    compute_x(2)
-    compute_g(2)
-    step(4)
-    compute_x(3)
-    compute_g(3)
-    sum_cores(2)
+    step(2, compute(0))
+    step(3, [P_(sum_cores, 0)] + compute(1))
+    step(4, [P_(sum_cores, 1), P_(sum_chips, 0)] + compute(2) + [P_(sum_cores, 2)])
+    for task in compute(3):
+        task()
     sum_chips(1)
     sum_cores(3)
     relay(hb, "h", 0)
     retile(xflat, y, xt)
     sum_chips(2)
     relay(hb, "h", 1)
+    retile(gflat, z, gt)
     sum_chips(3)
-    delta(3)
-    for g in (2, 1, 0):
+    for g in (3, 2, 1, 0):
         delta(g)
     relay(hb, "h", 2)
     for g in (0, 1, 2):
@@ -435,26 +454,27 @@
     all_home("d", 3)
     back_part((3,))
     ring_send("t", 0)
-    for g in (2, 1, 0):
-        relay(db, "d", g)
-    for g in (2, 1, 0):
-        all_home("d", g)
-    back_part((2, 1, 0))
+    relay(db, "d", 2)
+    relay(db, "d", 1)
+    relay(db, "d", 0)
+    all_home("d", 2)
+    back_part((2,))
     ring_send("m", 1)
     ring_send("t", 1)
-    tile_up(db, dtile)
-    lax.fori_loop(0, 18, one_up, jnp.int32(0))
-    store(gu, gu_hbm, 6)
+    all_home("d", 1)
+    all_home("d", 0)
+    back_part((1, 0))
     ring_send("m", 2)
     ring_send("t", 2)
+    tile_up(db, dtile)
     tile_up(hb, htile)
-    retile(gflat, z, gt)
+    up_some(0, 9)
     ring_send("m", 3)
     ring_send("t", 3)
-    lax.fori_loop(0, 18, one_down, jnp.int32(0))
-    store(gd, gd_hbm, 7)
+    up_some(9, 18)
     ring_end("m", ms2, mr2)
     ring_end("t", ts2, tr2)
+    down_some(0, 18)
 
     def finish(name, recv2, out):
         car, _, _, pos, cross, _, _ = outs[name]
@@ -478,16 +498,16 @@
     vmem = pl.BlockSpec(memory_space=pltpu.VMEM)
     hbm = pl.BlockSpec(memory_space=pltpu.HBM)
     V = pltpu.VMEM
-    return pl.pallas_call(
+    results = pl.pallas_call(
         kernel,
         out_shape=(
-            jax.ShapeDtypeStruct((4, 1536), BF),
-            jax.ShapeDtypeStruct((4, 1536), BF),
-            jax.ShapeDtypeStruct((1, 1, 18, 128, 128), F32),
-            jax.ShapeDtypeStruct((1, 1, 18, 128, 128), F32),
+            V((4, 1536), BF),
+            V((4, 1536), BF),
+            V((1, 1, 18, 128, 128), F32),
+            V((1, 1, 18, 128, 128), F32),
         ),
         in_specs=[hbm] * 6,
-        out_specs=(vmem, vmem, hbm, hbm),
+        out_specs=(vmem,) * 4,
         scratch_shapes=[
             V((4, 1536), BF),
             V((4, 1536), BF),
@@ -526,16 +546,26 @@
             V((384, 128), BF),
             V((8, 48, 128), BF),
             V((48, 128), F32),
-            V((18, 128, 128), F32),
-            V((18, 128, 128), F32),
             pltpu.SemaphoreType.DMA((N_COPIES,)),
             pltpu.SemaphoreType.DMA((N_COPIES,)),
             pltpu.SemaphoreType.DMA((8,)),
         ],
         compiler_params=pltpu.CompilerParams(
-            collective_id=0, has_side_effects=True, vmem_limit_bytes=56 * 1024 * 1024
+            collective_id=0, has_side_effects=True, vmem_limit_bytes=40 * 1024 * 1024
         ),
-    )(tokens, out_grad, up_tiles, down_tiles, up_slots, down_slots)
+    )(
+        *(
+            pltpu.with_memory_space_constraint(a, pltpu.HBM)
+            for a in (tokens, out_grad, up_tiles, down_tiles, up_slots, down_slots)
+        )
+    )
+    return pl.pallas_call(
+        write_out,
+        out_shape=tuple(jax.ShapeDtypeStruct(r.shape, r.dtype) for r in results),
+        in_specs=[vmem] * 4,
+        out_specs=(hbm,) * 4,
+        scratch_shapes=[pltpu.SemaphoreType.DMA((4,))],
+    )(*results)
 
 
 def solution(mesh):

time: 83.2 us -> 80.7 us (0.970)
  local copies, waits for them, and re-layouts: 6.12 us -> 3.23 us
    unnamed x6 -> x8, local copies, waits for them, and re-layouts: 6.12 us -> 3.23 us
    pallas_call x1 -> x2, Pallas kernels: 75.9 us -> 76.6 us  [the longest x1 73.5 us: per_device(): pl.pallas_call(kernel, out_shape=(V((4, 1536), BF), V((4, 1536), BF), V((...]
where the time goes in v3:
time: 80.7 us; the launch traced here: 80.5 us
  Pallas kernels  76.6 us (95%)
  local copies, waits for them, and re-layouts  3.23 us (4%)
    pallas_call x1, Pallas kernels, per_device(): pl.pallas_call(kernel, out_shape=(V((4, 1536), BF), V((4, 1536), BF), V((...  73.5 us
    unnamed x8, local copies, waits for them, and re-layouts  3.23 us
    pallas_call x1, Pallas kernels, per_device(): pl.pallas_call(write_out, out_shape=tuple((jax.ShapeDtypeStruct(r.shape,...  3.1 us

profile of v3, /device:TPU:6, one launch (start us, length us, event | category | flops | bytes accessed | tf_op | source)
XLA Modules:
  0.0 80.5 jit_solution(5158673118610923131)
XLA Ops:
  0.6 73.5 %shard_map.93 = (bf16[4,1536]{1,0:T(4,128)(2,1)S(1)}, bf16[4,1536]{1,0:T(4,128)(2,1)S(1)}, f32[1,1,18,128,128]{4,3,2,1,0:T(8,128)S(1)}, f32[1,1,18,128,128]{4,3,2,1,0:T(8,128)S(1)}) custom-call(bf16[4,1536]{1,0:T(4,128)(2,1)} %x_hbm.1, bf16[4,1536]{1,0:T(4,128)(2,1)} %g_hbm.1, bf16[1,1,18,128,128]{4,3,2,1,0:T(8,128)(2,1)} %ut_hbm.1, ...), custom_call_target="tpu_custom_call" | custom-call | tf_op jit(solution)/shard_map/pallas_call | solution.py:501
  74.2 0.0 copy-start
  74.2 1.0 %copy-done = f32[1,1,18,128,128]{4,3,2,1,0:T(8,128)} copy-done((f32[1,1,18,128,128]{4,3,2,1,0:T(8,128)}, f32[1,1,18,128,128]{4,3,2,1,0:T(8,128)S(1)}, u32[]{:S(2)}) %copy-start) | copy-done | bytes 1179672
  75.2 0.0 copy-start.1
  75.2 1.0 %copy-done.1 = f32[1,1,18,128,128]{4,3,2,1,0:T(8,128)} copy-done((f32[1,1,18,128,128]{4,3,2,1,0:T(8,128)}, f32[1,1,18,128,128]{4,3,2,1,0:T(8,128)S(1)}, u32[]{:S(2)}) %copy-start.1) | copy-done | bytes 1179672
  76.2 0.0 copy-start.2
  76.2 0.6 copy-done.2
  76.8 0.0 copy-start.3
  76.8 0.6 copy-done.3
  77.4 3.1 %shard_map.94 = (bf16[4,1536]{1,0:T(4,128)(2,1)}, bf16[4,1536]{1,0:T(4,128)(2,1)}, f32[1,1,18,128,128]{4,3,2,1,0:T(8,128)}, f32[1,1,18,128,128]{4,3,2,1,0:T(8,128)}) custom-call(bf16[4,1536]{1,0:T(4,128)(2,1)} %copy-done.2, bf16[4,1536]{1,0:T(4,128)(2,1)} %copy-done.3, f32[1,1,18,128,128]{4,3,2,1,0:T(8,128)} %copy-done, f32[1,1,18,128,128]{4,3,2,1,0:T(8,128)} %copy-done.1), custom_call_target="tpu_custom_call" | custom-call | tf_op jit(solution)/shard_map/pallas_call | solution.py:562
Async XLA Ops:
  74.2 1.0 %copy-start = (f32[1,1,18,128,128]{4,3,2,1,0:T(8,128)}, f32[1,1,18,128,128]{4,3,2,1,0:T(8,128)S(1)}, u32[]{:S(2)}) copy-start(f32[1,1,18,128,128]{4,3,2,1,0:T(8,128)S(1)} %get-tuple-element.10.c) | copy-start | bytes 3538948
  75.2 1.0 %copy-start.1 = (f32[1,1,18,128,128]{4,3,2,1,0:T(8,128)}, f32[1,1,18,128,128]{4,3,2,1,0:T(8,128)S(1)}, u32[]{:S(2)}) copy-start(f32[1,1,18,128,128]{4,3,2,1,0:T(8,128)S(1)} %get-tuple-element.11.d) | copy-start | bytes 3538948
  76.2 0.6 copy-start.2
  76.8 0.6 copy-start.3

commit v4 on v3

--- a/solution.py
+++ b/solution.py
@@ -16,6 +16,11 @@
 
 NEAR = (0, 1, 3, 2)
 FAR = (2, 3, 1, 0)
+ORDER = FAR
+SKIP = (2, 3)
+REACH = ((4, 3), (3, 4), (3, 3), (3, 3))
+SHORT = ()
+SUMS = ((4, 3),) * 4
 
 
 def gelu_both(v):
@@ -72,8 +77,9 @@
         low = lax.rem(pos, 2)
         return pair(pos, k) * 2 + (1 - low if b else low)
 
-    others = [(k, b) for k in NEAR for b in (0, 1) if (k, b) != (0, 0)]
+    others = [(k, b) for k in FAR for b in (0, 1) if (k, b) != (0, 0)]
     xpeer = [(hid, lax.rem(xx + o, 4) * 2 + c) for o in (1, 2, 3)]
+    xcross = [(hid, lax.rem(xx + o, 4) * 2 + 1 - c) for o in (1, 2, 3)]
     partner = (hid, xx * 2 + 1 - c)
 
     counter = [0]
@@ -93,7 +99,7 @@
 
     barrier = pltpu.get_barrier_semaphore()
     peers = [at(z, mate(y, k, b)) for k, b in others] + [at(mate(z, k, b), y) for k, b in others]
-    peers += xpeer + [partner]
+    peers += xpeer + xcross + [partner]
     for dev in peers:
         pl.semaphore_signal(barrier, inc=1, device_id=dev, device_id_type=MESH)
 
@@ -150,8 +156,8 @@
     build(ds, dt, w2, 6, 12)
 
     axes = {
-        "x": (xcar, z, y, at(z + 1, y), at(z - 1, y)),
-        "g": (gcar, y, z, at(z, y + 1), at(z, y - 1)),
+        "x": (xcar, z, y, lambda d: at(z + d, y)),
+        "g": (gcar, y, z, lambda d: at(z, y + d)),
     }
     ring = {}
 
@@ -168,22 +174,30 @@
         run(tasks, share)
         for k in NEAR:
             for name in ("x", "g"):
-                car, pos, cross, right, left = axes[name]
+                car, pos, cross, dev = axes[name]
+                span = pl.ds(pair(cross, k) * 2, 2)
+
+                def forward(slab, hops, key):
+                    ref = car.at[up8(slab), span]
+                    ring[(name, k) + key] = rcopy(ref, ref, dev(hops))
+
                 if s == 0:
                     for b in (0, 1):
                         if (k, b) != (0, 0):
                             first[name, k, b].wait_recv()
                 else:
-                    ring[name, s - 1, k, "r"].wait_recv()
-                    if s < 4:
-                        ring[name, s - 1, k, "l"].wait_recv()
-                span = pl.ds(pair(cross, k) * 2, 2)
-                if s < 4:
-                    ref = car.at[up8(pos - s), span]
-                    ring[name, s, k, "r"] = rcopy(ref, ref, right)
-                if s < 3:
-                    ref = car.at[up8(pos + s), span]
-                    ring[name, s, k, "l"] = rcopy(ref, ref, left)
+                    for way in (0, 1):
+                        if s <= REACH[k][way]:
+                            ring[name, k, s - 1, way].wait_recv()
+                    if s == 4 and k in SKIP:
+                        ring[name, k, 2, 2].wait_recv()
+                if s == 2 and k in SKIP:
+                    way = 1 if k == 2 else -1
+                    forward(pos - 2 * way, 2 * way, (2, 2))
+                for way in (0, 1):
+                    if s < REACH[k][way]:
+                        sign = 1 - 2 * way
+                        forward(pos - sign * s, sign, (s, way))
             run(tasks, share)
 
     def widen(car, pos, flat, off):
@@ -221,26 +235,27 @@
         if q == 2:
             core[g, a] = rcopy(part.at[g, 1 - c, a], rcore.at[g, a], partner)
 
-    def compute(g):
-        tasks = []
-        for a, car, pos, flat, dst in ((0, xcar, z, xflat, xs), (1, gcar, y, gflat, gs)):
-            for off in offsets(g):
-                tasks.append(functools.partial(widen, car, pos, flat, off))
-            for t in range(4):
-                tasks.append(functools.partial(unpack, pos, flat, dst, g, (3 * t, 3 * t + 1, 3 * t + 2)))
-            for q in range(3):
-                tasks.append(functools.partial(product, a, g, q))
-        return tasks
-
-    def sum_cores(g):
-        for a in range(2):
-            core[g, a].wait_recv()
-            total = part[g, c, a] + rcore[g, a]
-            rcore[g, a] = total
-            for i in range(4):
-                sb[g, i, a] = total[i * 16 : (i + 1) * 16].astype(BF)
+    def compute(g, a):
+        car, pos, flat, dst = ((xcar, z, xflat, xs), (gcar, y, gflat, gs))[a]
+        tasks = [functools.partial(widen, car, pos, flat, off) for off in offsets(g)]
+        for t in range(4):
+            tasks.append(
+                functools.partial(unpack, pos, flat, dst, g, (3 * t, 3 * t + 1, 3 * t + 2))
+            )
+        return tasks + [functools.partial(product, a, g, q) for q in range(3)]
+
+    def compute_now(g, a):
+        for task in compute(g, a):
+            task()
+
+    def sum_cores(g, a):
+        core[g, a].wait_recv()
+        total = part[g, c, a] + rcore[g, a]
+        rcore[g, a] = total
+        for i in range(4):
+            sb[g, i, a] = total[i * 16 : (i + 1) * 16].astype(BF)
         for dev, o in zip(xpeer, (1, 2, 3)):
-            over[g, o] = rcopy(sb.at[g, lax.rem(xx + o, 4)], rx.at[g, o], dev)
+            over[g, a, o] = rcopy(sb.at[g, lax.rem(xx + o, 4), a], rx.at[g, o, a], dev)
 
     def mine(buf, g, i):
         return buf.at[
@@ -251,7 +266,8 @@
 
     def send_home(buf, name, g):
         ref = mine(buf, g, xx)
-        back_home[name, g] = [rcopy(ref, ref, dev) for dev in xpeer] + [rcopy(ref, ref, partner)]
+        devs = xpeer + [partner] + (xcross if g == 3 else [])
+        back_home[name, g] = [rcopy(ref, ref, dev) for dev in devs]
 
     def relay(buf, name, g):
         for n, o in enumerate((1, 2, 3)):
@@ -260,30 +276,33 @@
             back_home[name, g].append(rcopy(ref, ref, partner))
 
     def all_home(name, g):
-        for cp in back_home[name, g][3:]:
+        for cp in back_home[name, g][0 if g == 3 else 3 :]:
             cp.wait_recv()
 
-    def sum_chips(g):
-        acc = [rcore[g, a, pl.ds(pl.multiple_of(xx * 16, 16), 16), :] for a in range(2)]
+    def sum_chips(g, a):
+        acc = rcore[g, a, pl.ds(pl.multiple_of(xx * 16, 16), 16), :]
         for o in (1, 2, 3):
-            over[g, o].wait_recv()
-            acc = [acc[a] + rx[g, o, a].astype(F32) for a in range(2)]
-        value, slope = gelu_both(acc[0])
+            over[g, a, o].wait_recv()
+            acc = acc + rx[g, o, a].astype(F32)
+        return acc
+
+    def lay(buf, val, pos, g):
+        for n, off in enumerate(offsets(g)):
+            d = up8(pos + off)
+            for t in range(3):
+                buf[t, pl.ds(pl.multiple_of(d * 8, 8), 8), :] = val[
+                    n * 8 : (n + 1) * 8, t * 128 : (t + 1) * 128
+                ]
+
+    def hidden(g):
+        value, slope = gelu_both(sum_chips(g, 0))
         ref = mine(hb, g, xx)
         ref[...] = value.astype(BF)
         send_home(hb, "h", g)
-        for n, off in enumerate(offsets(g)):
-            dz, dy = up8(z + off), up8(y + off)
-            for t in range(3):
-                lanes = slice(t * 128, (t + 1) * 128)
-                slopes[t, pl.ds(pl.multiple_of(dz * 8, 8), 8), :] = slope[
-                    n * 8 : (n + 1) * 8, lanes
-                ]
-                backs[t, pl.ds(pl.multiple_of(dy * 8, 8), 8), :] = acc[1][
-                    n * 8 : (n + 1) * 8, lanes
-                ]
+        lay(slopes, slope, z, g)
 
     def delta(g):
+        lay(backs, sum_chips(g, 1), y, g)
         rows = []
         for off in offsets(g):
             dy = up8(y + off)
@@ -334,7 +353,8 @@
             pack(val[:, 128:], 2 * q + 1, mcar, z, groups)
             return carry
 
-        lax.fori_loop(0, 6, cols, jnp.int32(0))
+        for q in range(6):
+            cols(q, 0)
 
     def back_part(groups):
         lhs = jnp.concatenate([db[g] for g in groups], axis=0)
@@ -350,75 +370,109 @@
             pack(val[:, 128:], 2 * q + 1, tcar, y, groups)
             return carry
 
-        lax.fori_loop(0, 6, cols, jnp.int32(0))
+        for q in range(6):
+            cols(q, 0)
 
     outs = {
-        "m": (mcar, msend, mrecv, z, y, at(z + 1, y), at(z - 1, y)),
-        "t": (tcar, tsend, trecv, y, z, at(z, y + 1), at(z, y - 1)),
+        "m": (mcar, msend, mrecv, z, y, lambda d: at(z + d, y), ms2, mr2),
+        "t": (tcar, tsend, trecv, y, z, lambda d: at(z, y + d), ts2, tr2),
     }
     rsum = {}
-
-    def ring_send(name, s):
-        car, send, recv, pos, cross, right, left = outs[name]
-        for k in FAR:
-            at_rows = pair(cross, k) * 96
-            span = pl.ds(pl.multiple_of(at_rows, 96), 96)
-            for w, dev, d in ((0, right, pos + 4 - s), (1, left, pos - 3 + s)):
-                if w == 1 and s == 3:
-                    continue
-                val = car[pl.ds(pl.multiple_of(up8(d) * 384 + at_rows, 96), 96), :]
-                if s > 0:
-                    rsum[name, s - 1, k, w].wait_recv()
-                    val = val + recv[w, s - 1, span, :].astype(F32)
-                send[w, s, span, :] = val.astype(BF)
-                rsum[name, s, k, w] = rcopy(
-                    send.at[w, s, span, :], recv.at[w, s, span, :], dev
-                )
-
     last = {}
 
-    def ring_end(name, send2, recv2):
-        car, send, recv, pos, cross, right, left = outs[name]
-        for k in FAR:
-            at_rows = pair(cross, k) * 96
-            span = pl.ds(pl.multiple_of(at_rows, 96), 96)
-            rsum[name, 3, k, 0].wait_recv()
-            rsum[name, 2, k, 1].wait_recv()
-            here = pl.ds(pl.multiple_of(pos * 384 + at_rows, 96), 96)
-            val = car[here, :] + recv[0, 3, span, :].astype(F32) + recv[1, 2, span, :].astype(F32)
-            car[here, :] = val
-            send2[span, :] = val.astype(BF)
-            for b in (0, 1):
-                if (k, b) == (0, 0):
-                    continue
-                to = mate(cross, k, b)
-                dev = at(pos, to) if name == "m" else at(to, pos)
-                n = 2 * k + b
-                last[name, k, b] = rcopy(
-                    send2.at[pl.ds(pl.multiple_of(to * 48, 48), 48), :], recv2.at[n], dev
-                )
+    def block(name, k, d):
+        car, pos, cross = outs[name][0], outs[name][3], outs[name][4]
+        return pl.ds(pl.multiple_of(up8(pos + d) * 384 + pair(cross, k) * 96, 96), 96)
+
+    def span_of(name, k):
+        return pl.ds(pl.multiple_of(pair(outs[name][4], k) * 96, 96), 96)
+
+    def got(name, k, way, s):
+        rsum[name, k, way, s].wait_recv()
+        return outs[name][2][way, s, span_of(name, k), :].astype(F32)
+
+    def ring_send(name, k, s):
+        car, send, recv, pos, cross, dev, _, _ = outs[name]
+        span = span_of(name, k)
+
+        def push(val, way, hops):
+            send[way, s, span, :] = val.astype(BF)
+            rsum[name, k, way, s] = rcopy(
+                send.at[way, s, span, :], recv.at[way, s, span, :], dev(hops)
+            )
+
+        far_way = SHORT.index(k) if k in SHORT else None
+        if s == 0 and k in SHORT:
+            push(car[block(name, k, 4), :], 2, 2 - 4 * far_way)
+        for way in (0, 1):
+            reach = SUMS[k][way] - s
+            if reach < 1:
+                continue
+            val = car[block(name, k, reach if way == 0 else -reach), :]
+            if s > 0:
+                val = val + got(name, k, way, s - 1)
+            if s == 1 and far_way == way:
+                val = val + got(name, k, 2, 0)
+            push(val, way, 1 - 2 * way)
+
+    def ring_end(name, k):
+        car, _, _, pos, cross, _, send2, recv2 = outs[name]
+        span = span_of(name, k)
+        here = block(name, k, 0)
+        val = car[here, :] + got(name, k, 0, SUMS[k][0] - 1) + got(name, k, 1, SUMS[k][1] - 1)
+        car[here, :] = val
+        send2[span, :] = val.astype(BF)
+        for b in (0, 1):
+            if (k, b) == (0, 0):
+                continue
+            to = mate(cross, k, b)
+            dev = at(pos, to) if name == "m" else at(to, pos)
+            last[name, k, b] = rcopy(
+                send2.at[pl.ds(pl.multiple_of(to * 48, 48), 48), :], recv2.at[2 * k + b], dev
+            )
+
+    def ring_step(s, names=("m", "t"), pairs=ORDER, tasks=()):
+        tasks = list(tasks)
+        share = -(-len(tasks) // len(pairs))
+        for k in pairs:
+            for name in names:
+                if s == 3 and k in SHORT:
+                    ring_end(name, k)
+                elif s == 4:
+                    ring_end(name, k)
+                else:
+                    ring_send(name, k, s)
+            run(tasks, share)
 
     def up_some(lo, hi):
-        def one(n, carry):
+        def one(n):
             slot = us[0, 0, n]
             lhs, rhs = xt[lax.div(slot, 6)], dtile[lax.rem(slot, 6)]
             gu[0, 0, n] = lax.dot_general(
                 lhs, rhs, (((0,), (0,)), ((), ())), preferred_element_type=F32
             )
+
+        def six(t, carry):
+            for n in range(6):
+                one(lo + 6 * t + n)
             return carry
 
-        lax.fori_loop(lo, hi, one, jnp.int32(0))
+        lax.fori_loop(0, (hi - lo) // 6, six, jnp.int32(0))
 
     def down_some(lo, hi):
-        def one(n, carry):
+        def one(n):
             slot = ds[0, 0, n]
             lhs, rhs = htile[lax.div(slot, 12)], gt[lax.rem(slot, 12)]
             gd[0, 0, n] = lax.dot_general(
                 lhs, rhs, (((0,), (0,)), ((), ())), preferred_element_type=F32
             )
+
+        def six(t, carry):
+            for n in range(6):
+                one(lo + 6 * t + n)
             return carry
 
-        lax.fori_loop(lo, hi, one, jnp.int32(0))
+        lax.fori_loop(0, (hi - lo) // 6, six, jnp.int32(0))
 
     def tile_up(buf, dst):
         for b in range(6):
@@ -427,57 +481,65 @@
     P_ = functools.partial
     step(0)
     step(1)
-    step(2, compute(0))
-    step(3, [P_(sum_cores, 0)] + compute(1))
-    step(4, [P_(sum_cores, 1), P_(sum_chips, 0)] + compute(2) + [P_(sum_cores, 2)])
-    for task in compute(3):
-        task()
-    sum_chips(1)
-    sum_cores(3)
+    step(2, compute(0, 0))
+    todo = compute(1, 0)
+    step(3, todo[:5] + [P_(sum_cores, 0, 0)] + todo[5:])
+    todo = compute(2, 0)
+    step(4, todo[:5] + [P_(sum_cores, 1, 0)] + todo[5:])
+    compute_now(3, 0)
+    sum_cores(2, 0)
+    compute_now(3, 1)
+    sum_cores(3, 0)
+    compute_now(2, 1)
+    sum_cores(3, 1)
+    hidden(0)
+    compute_now(1, 1)
+    sum_cores(2, 1)
+    hidden(1)
+    compute_now(0, 1)
+    sum_cores(1, 1)
+    hidden(2)
+    sum_cores(0, 1)
     relay(hb, "h", 0)
+    hidden(3)
+    delta(3)
+    relay(hb, "h", 1)
+    delta(2)
     retile(xflat, y, xt)
-    sum_chips(2)
-    relay(hb, "h", 1)
-    retile(gflat, z, gt)
-    sum_chips(3)
-    for g in (3, 2, 1, 0):
-        delta(g)
+    delta(1)
+    delta(0)
     relay(hb, "h", 2)
-    for g in (0, 1, 2):
-        all_home("h", g)
-    mixed_part((0, 1, 2))
-    relay(hb, "h", 3)
-    relay(db, "d", 3)
+    all_home("h", 2)
+    mixed_part((2,))
     all_home("h", 3)
     mixed_part((3,))
-    ring_send("m", 0)
+    ring_step(0, names=("m",))
     all_home("d", 3)
     back_part((3,))
-    ring_send("t", 0)
+    ring_step(0, names=("t",))
     relay(db, "d", 2)
+    all_home("d", 2)
+    back_part((2,))
+    ring_step(1)
     relay(db, "d", 1)
     relay(db, "d", 0)
-    all_home("d", 2)
-    back_part((2,))
-    ring_send("m", 1)
-    ring_send("t", 1)
-    all_home("d", 1)
-    all_home("d", 0)
+    for g in (1, 0):
+        all_home("h", g)
+        all_home("d", g)
+    mixed_part((1, 0))
     back_part((1, 0))
-    ring_send("m", 2)
-    ring_send("t", 2)
+    ring_step(2)
     tile_up(db, dtile)
+    up_some(0, 6)
+    ring_step(3)
+    up_some(6, 18)
+    ring_step(4)
     tile_up(hb, htile)
-    up_some(0, 9)
-    ring_send("m", 3)
-    ring_send("t", 3)
-    up_some(9, 18)
-    ring_end("m", ms2, mr2)
-    ring_end("t", ts2, tr2)
+    retile(gflat, z, gt)
     down_some(0, 18)
 
     def finish(name, recv2, out):
-        car, _, _, pos, cross, _, _ = outs[name]
+        car, _, _, pos, cross, _, _, _ = outs[name]
         acc = car[pl.ds(pl.multiple_of(pos * 384 + cross * 48, 48), 48), :]
         for k, b in others:
             last[name, k, b].wait_recv()
@@ -491,7 +553,7 @@
     drain(sent, stores)
 
 
-N_COPIES = 14 + 56 + 8 + 12 + 56 + 56 + 14
+N_COPIES = 14 + 56 + 8 + 24 + 56 + 56 + 14 + 16
 
 
 def per_device(tokens, out_grad, up_tiles, down_tiles, up_slots, down_slots):
@@ -537,10 +599,10 @@
             V((6, 256, 128), BF),
             V((3072, 128), F32),
             V((3072, 128), F32),
-            V((2, 4, 384, 128), BF),
-            V((2, 4, 384, 128), BF),
-            V((2, 4, 384, 128), BF),
-            V((2, 4, 384, 128), BF),
+            V((3, 4, 384, 128), BF),
+            V((3, 4, 384, 128), BF),
+            V((3, 4, 384, 128), BF),
+            V((3, 4, 384, 128), BF),
             V((384, 128), BF),
             V((8, 48, 128), BF),
             V((384, 128), BF),
@@ -565,7 +627,8 @@
         in_specs=[vmem] * 4,
         out_specs=(hbm,) * 4,
         scratch_shapes=[pltpu.SemaphoreType.DMA((4,))],
-    )(*results)
+        compiler_params=pltpu.CompilerParams(vmem_limit_bytes=4 * 1024 * 1024),
+    )(*(pltpu.with_memory_space_constraint(r, pltpu.VMEM) for r in results))
 
 
 def solution(mesh):

time: 80.7 us -> 72.2 us (0.89)
  Pallas kernels: 76.6 us -> 70.8 us
  local copies, waits for them, and re-layouts: 3.23 us -> 0 us
    pallas_call x1, Pallas kernels: 73.5 us -> 69.4 us  [per_device(): pl.pallas_call(kernel, out_shape=(V((4, 1536), BF), V((4, 1536), BF), V((...]
    unnamed x8 -> x0, local copies, waits for them, and re-layouts: 3.23 us -> none
    pallas_call x1, Pallas kernels: 3.1 us -> 1.45 us  [per_device(): pl.pallas_call(write_out, out_shape=tuple((jax.ShapeDtypeStruct(r.shape,...]
where the time goes in v4:
time: 72.2 us; the launch traced here: 71.4 us
  Pallas kernels  70.8 us (98%)
    pallas_call x1, Pallas kernels, per_device(): pl.pallas_call(kernel, out_shape=(V((4, 1536), BF), V((4, 1536), BF), V((...  69.4 us
    pallas_call x1, Pallas kernels, per_device(): pl.pallas_call(write_out, out_shape=tuple((jax.ShapeDtypeStruct(r.shape,...  1.45 us

profile of v4, /device:TPU:6, one launch (start us, length us, event | category | flops | bytes accessed | tf_op | source)
XLA Modules:
  0.0 71.4 jit_solution(7485465871878403869)
XLA Ops:
  0.6 69.4 %shard_map.93 = (bf16[4,1536]{1,0:T(4,128)(2,1)S(1)}, bf16[4,1536]{1,0:T(4,128)(2,1)S(1)}, f32[1,1,18,128,128]{4,3,2,1,0:T(8,128)S(1)}, f32[1,1,18,128,128]{4,3,2,1,0:T(8,128)S(1)}) custom-call(bf16[4,1536]{1,0:T(4,128)(2,1)} %x_hbm.1, bf16[4,1536]{1,0:T(4,128)(2,1)} %g_hbm.1, bf16[1,1,18,128,128]{4,3,2,1,0:T(8,128)(2,1)} %ut_hbm.1, ...), custom_call_target="tpu_custom_call" | custom-call | tf_op jit(solution)/shard_map/pallas_call | solution.py:563
  70.0 1.4 %shard_map.94 = (bf16[4,1536]{1,0:T(4,128)(2,1)}, bf16[4,1536]{1,0:T(4,128)(2,1)}, f32[1,1,18,128,128]{4,3,2,1,0:T(8,128)}, f32[1,1,18,128,128]{4,3,2,1,0:T(8,128)}) custom-call(bf16[4,1536]{1,0:T(4,128)(2,1)S(1)} %get-tuple-element.8.a, bf16[4,1536]{1,0:T(4,128)(2,1)S(1)} %get-tuple-element.9.b, f32[1,1,18,128,128]{4,3,2,1,0:T(8,128)S(1)} %get-tuple-element.10.c, ...), custom_call_target="tpu_custom_call" | custom-call | tf_op jit(solution)/shard_map/pallas_call | solution.py:624

commit v5 on v4

--- a/solution.py
+++ b/solution.py
@@ -163,6 +163,11 @@
 
     def offsets(g):
         return (-g, g + 1)
+
+    def settle(keep=0):
+        for cp in sent[: len(sent) - keep]:
+            cp.wait_send()
+        del sent[: len(sent) - keep]
 
     def run(tasks, share):
         for _ in range(min(len(tasks), share)):
@@ -508,9 +513,11 @@
     retile(xflat, y, xt)
     delta(1)
     delta(0)
+    for g in (1, 0):
+        all_home("h", g)
+    mixed_part((1, 0))
+    settle(60)
     relay(hb, "h", 2)
-    all_home("h", 2)
-    mixed_part((2,))
     all_home("h", 3)
     mixed_part((3,))
     ring_step(0, names=("m",))
@@ -518,17 +525,18 @@
     back_part((3,))
     ring_step(0, names=("t",))
     relay(db, "d", 2)
+    all_home("h", 2)
+    mixed_part((2,))
     all_home("d", 2)
     back_part((2,))
     ring_step(1)
     relay(db, "d", 1)
     relay(db, "d", 0)
     for g in (1, 0):
-        all_home("h", g)
         all_home("d", g)
-    mixed_part((1, 0))
     back_part((1, 0))
     ring_step(2)
+    settle(40)
     tile_up(db, dtile)
     up_some(0, 6)
     ring_step(3)
@@ -537,6 +545,7 @@
     tile_up(hb, htile)
     retile(gflat, z, gt)
     down_some(0, 18)
+    settle(14)
 
     def finish(name, recv2, out):
         car, _, _, pos, cross, _, _, _ = outs[name]

time: 72.2 us -> 71.5 us (level)
  Pallas kernels: 70.8 us -> 70 us
    pallas_call x1, Pallas kernels: 69.4 us -> 68.6 us  [per_device(): pl.pallas_call(kernel, out_shape=(V((4, 1536), BF), V((4, 1536), BF), V((...]
where the time goes in v5:
time: 71.5 us; the launch traced here: 70.7 us
  Pallas kernels  70 us (98%)
    pallas_call x1, Pallas kernels, per_device(): pl.pallas_call(kernel, out_shape=(V((4, 1536), BF), V((4, 1536), BF), V((...  68.6 us
    pallas_call x1, Pallas kernels, per_device(): pl.pallas_call(write_out, out_shape=tuple((jax.ShapeDtypeStruct(r.shape,...  1.45 us

profile of v5, /device:TPU:6, one launch (start us, length us, event | category | flops | bytes accessed | tf_op | source)
XLA Modules:
  0.0 70.7 jit_solution(4611946769631835412)
XLA Ops:
  0.6 68.6 %shard_map.93 = (bf16[4,1536]{1,0:T(4,128)(2,1)S(1)}, bf16[4,1536]{1,0:T(4,128)(2,1)S(1)}, f32[1,1,18,128,128]{4,3,2,1,0:T(8,128)S(1)}, f32[1,1,18,128,128]{4,3,2,1,0:T(8,128)S(1)}) custom-call(bf16[4,1536]{1,0:T(4,128)(2,1)} %x_hbm.1, bf16[4,1536]{1,0:T(4,128)(2,1)} %g_hbm.1, bf16[1,1,18,128,128]{4,3,2,1,0:T(8,128)(2,1)} %ut_hbm.1, ...), custom_call_target="tpu_custom_call" | custom-call | tf_op jit(solution)/shard_map/pallas_call | solution.py:572
  69.2 1.4 %shard_map.94 = (bf16[4,1536]{1,0:T(4,128)(2,1)}, bf16[4,1536]{1,0:T(4,128)(2,1)}, f32[1,1,18,128,128]{4,3,2,1,0:T(8,128)}, f32[1,1,18,128,128]{4,3,2,1,0:T(8,128)}) custom-call(bf16[4,1536]{1,0:T(4,128)(2,1)S(1)} %get-tuple-element.8.a, bf16[4,1536]{1,0:T(4,128)(2,1)S(1)} %get-tuple-element.9.b, f32[1,1,18,128,128]{4,3,2,1,0:T(8,128)S(1)} %get-tuple-element.10.c, ...), custom_call_target="tpu_custom_call" | custom-call | tf_op jit(solution)/shard_map/pallas_call | solution.py:633

commit v6 on v5

--- a/solution.py
+++ b/solution.py
@@ -17,8 +17,8 @@
 NEAR = (0, 1, 3, 2)
 FAR = (2, 3, 1, 0)
 ORDER = FAR
-SKIP = (2, 3)
-REACH = ((4, 3), (3, 4), (3, 3), (3, 3))
+SKIP = (1, 2, 3)
+REACH = ((4, 3), (3, 3), (3, 3), (3, 3))
 SHORT = ()
 SUMS = ((4, 3),) * 4
 
@@ -77,7 +77,7 @@
         low = lax.rem(pos, 2)
         return pair(pos, k) * 2 + (1 - low if b else low)
 
-    others = [(k, b) for k in FAR for b in (0, 1) if (k, b) != (0, 0)]
+    others = [(k, b) for k in NEAR for b in (0, 1) if (k, b) != (0, 0)]
     xpeer = [(hid, lax.rem(xx + o, 4) * 2 + c) for o in (1, 2, 3)]
     xcross = [(hid, lax.rem(xx + o, 4) * 2 + 1 - c) for o in (1, 2, 3)]
     partner = (hid, xx * 2 + 1 - c)
@@ -197,7 +197,7 @@
                     if s == 4 and k in SKIP:
                         ring[name, k, 2, 2].wait_recv()
                 if s == 2 and k in SKIP:
-                    way = 1 if k == 2 else -1
+                    way = -1 if k == 3 else 1
                     forward(pos - 2 * way, 2 * way, (2, 2))
                 for way in (0, 1):
                     if s < REACH[k][way]:
@@ -510,7 +510,6 @@
     delta(3)
     relay(hb, "h", 1)
     delta(2)
-    retile(xflat, y, xt)
     delta(1)
     delta(0)
     for g in (1, 0):
@@ -537,13 +536,14 @@
     back_part((1, 0))
     ring_step(2)
     settle(40)
+    retile(xflat, y, xt)
+    ring_step(3)
     tile_up(db, dtile)
-    up_some(0, 6)
-    ring_step(3)
-    up_some(6, 18)
+    up_some(0, 12)
     ring_step(4)
     tile_up(hb, htile)
     retile(gflat, z, gt)
+    up_some(12, 18)
     down_some(0, 18)
     settle(14)
 

time: 71.5 us -> 70.8 us (level)
  no operation moved by 1% of the time
where the time goes in v6:
time: 70.8 us; the launch traced here: 70.3 us
  Pallas kernels  69.6 us (98%)
    pallas_call x1, Pallas kernels, per_device(): pl.pallas_call(kernel, out_shape=(V((4, 1536), BF), V((4, 1536), BF), V((...  68.2 us
    pallas_call x1, Pallas kernels, per_device(): pl.pallas_call(write_out, out_shape=tuple((jax.ShapeDtypeStruct(r.shape,...  1.45 us

profile of v6, /device:TPU:6, one launch (start us, length us, event | category | flops | bytes accessed | tf_op | source)
XLA Modules:
  0.0 70.3 jit_solution(12995867441168105715)
XLA Ops:
  0.6 68.2 %shard_map.93 = (bf16[4,1536]{1,0:T(4,128)(2,1)S(1)}, bf16[4,1536]{1,0:T(4,128)(2,1)S(1)}, f32[1,1,18,128,128]{4,3,2,1,0:T(8,128)S(1)}, f32[1,1,18,128,128]{4,3,2,1,0:T(8,128)S(1)}) custom-call(bf16[4,1536]{1,0:T(4,128)(2,1)} %x_hbm.1, bf16[4,1536]{1,0:T(4,128)(2,1)} %g_hbm.1, bf16[1,1,18,128,128]{4,3,2,1,0:T(8,128)(2,1)} %ut_hbm.1, ...), custom_call_target="tpu_custom_call" | custom-call | tf_op jit(solution)/shard_map/pallas_call | solution.py:572
  68.8 1.4 %shard_map.94 = (bf16[4,1536]{1,0:T(4,128)(2,1)}, bf16[4,1536]{1,0:T(4,128)(2,1)}, f32[1,1,18,128,128]{4,3,2,1,0:T(8,128)}, f32[1,1,18,128,128]{4,3,2,1,0:T(8,128)}) custom-call(bf16[4,1536]{1,0:T(4,128)(2,1)S(1)} %get-tuple-element.8.a, bf16[4,1536]{1,0:T(4,128)(2,1)S(1)} %get-tuple-element.9.b, f32[1,1,18,128,128]{4,3,2,1,0:T(8,128)S(1)} %get-tuple-element.10.c, ...), custom_call_target="tpu_custom_call" | custom-call | tf_op jit(solution)/shard_map/pallas_call | solution.py:633

commit v7 on v6

--- a/solution.py
+++ b/solution.py
@@ -436,18 +436,17 @@
                 send2.at[pl.ds(pl.multiple_of(to * 48, 48), 48), :], recv2.at[2 * k + b], dev
             )
 
-    def ring_step(s, names=("m", "t"), pairs=ORDER, tasks=()):
-        tasks = list(tasks)
-        share = -(-len(tasks) // len(pairs))
-        for k in pairs:
-            for name in names:
-                if s == 3 and k in SHORT:
-                    ring_end(name, k)
-                elif s == 4:
-                    ring_end(name, k)
-                else:
-                    ring_send(name, k, s)
-            run(tasks, share)
+    def ring_step(s, names=("m", "t"), pairs=ORDER):
+        turns = sorted(
+            (n + 2 * names.index(name), names.index(name), name, k)
+            for n, k in enumerate(pairs)
+            for name in names
+        )
+        for _, _, name, k in turns:
+            if s == 4:
+                ring_end(name, k)
+            else:
+                ring_send(name, k, s)
 
     def up_some(lo, hi):
         def one(n):

time: 70.8 us -> 72.3 us (1.021)
  Pallas kernels: 69.6 us -> 70.8 us
    pallas_call x1, Pallas kernels: 68.2 us -> 69.4 us  [per_device(): pl.pallas_call(kernel, out_shape=(V((4, 1536), BF), V((4, 1536), BF), V((...]
where the time goes in v7:
time: 72.3 us; the launch traced here: 71.5 us
  Pallas kernels  70.8 us (98%)
    pallas_call x1, Pallas kernels, per_device(): pl.pallas_call(kernel, out_shape=(V((4, 1536), BF), V((4, 1536), BF), V((...  69.4 us
    pallas_call x1, Pallas kernels, per_device(): pl.pallas_call(write_out, out_shape=tuple((jax.ShapeDtypeStruct(r.shape,...  1.45 us

profile of v7, /device:TPU:6, one launch (start us, length us, event | category | flops | bytes accessed | tf_op | source)
XLA Modules:
  0.0 71.5 jit_solution(10323152912936090789)
XLA Ops:
  0.6 69.4 %shard_map.93 = (bf16[4,1536]{1,0:T(4,128)(2,1)S(1)}, bf16[4,1536]{1,0:T(4,128)(2,1)S(1)}, f32[1,1,18,128,128]{4,3,2,1,0:T(8,128)S(1)}, f32[1,1,18,128,128]{4,3,2,1,0:T(8,128)S(1)}) custom-call(bf16[4,1536]{1,0:T(4,128)(2,1)} %x_hbm.1, bf16[4,1536]{1,0:T(4,128)(2,1)} %g_hbm.1, bf16[1,1,18,128,128]{4,3,2,1,0:T(8,128)(2,1)} %ut_hbm.1, ...), custom_call_target="tpu_custom_call" | custom-call | tf_op jit(solution)/shard_map/pallas_call | solution.py:571
  70.0 1.4 %shard_map.94 = (bf16[4,1536]{1,0:T(4,128)(2,1)}, bf16[4,1536]{1,0:T(4,128)(2,1)}, f32[1,1,18,128,128]{4,3,2,1,0:T(8,128)}, f32[1,1,18,128,128]{4,3,2,1,0:T(8,128)}) custom-call(bf16[4,1536]{1,0:T(4,128)(2,1)S(1)} %get-tuple-element.8.a, bf16[4,1536]{1,0:T(4,128)(2,1)S(1)} %get-tuple-element.9.b, f32[1,1,18,128,128]{4,3,2,1,0:T(8,128)S(1)} %get-tuple-element.10.c, ...), custom_call_target="tpu_custom_call" | custom-call | tf_op jit(solution)/shard_map/pallas_call | solution.py:632
